TPU v7x, 32 devices: a whole 2x2x4 slice. The times are simulated.
32 devices in a mesh: dp: 8 (over z, y), tensor: 4 (over x, core).
Axes of the slice: x: 2, y: 2, z: 4, core: 2. Of those that a mesh axis runs over, the one named last changes fastest.
Arguments:
- tokens: bfloat16 [1024, 2048], P('dp', 'tensor'), may hold values from -6 to 6
- cotangent: bfloat16 [1024, 2048], P('dp', 'tensor'), may hold values from -6 to 6
- pair_ids: int32 [1024], P('dp'), may hold values from 0 to 99, as said below
- up_mask: int32 [100, 16, 64], P(None, None, 'tensor'), may hold values 0 or 1
- down_mask: int32 [100, 64, 16], P(None, 'tensor'), may hold values 0 or 1
- up_weight: bfloat16 [2048, 8192], P(None, 'tensor'), may hold values from -0.125 to 0.125
- down_weight: bfloat16 [8, 8192, 2048], P('dp', 'tensor'), may hold values from -0.0625 to 0.0625
Outputs:
- mixed: bfloat16 [1024, 2048], P('dp', 'tensor')
- token_grads: bfloat16 [1024, 2048], P('dp', 'tensor')
Inputs may be any that keep to these rules, and one draw needn't show every extreme that they name: `pair_ids`: within each aligned block of 128 tokens (the tokens of one index of dp) at most 24 tokens belong to one language group; in every draw 1 group hold exactly 24 tokens of every block.
All inputs are finite; a program needn't handle non-finite values. No bound on the sum of `up_mask` or of `down_mask` on one device may be relied on, other than what follows from the above.
Results may differ from a plain program's by a relative error of at most 0.014.
Values may be sent and summed in bfloat16 or wider, within the bound.
A program may use at most 128 MiB of HBM per device.

v0:
```python
import jax
import jax.numpy as jnp
from jax import lax
from jax.sharding import PartitionSpec as P

BLOCK = 128


def as_sent(x):

    def short(part):
        return part.astype(jnp.bfloat16) if part.dtype == jnp.float32 else part

    return jax.tree.map(short, x)


def row_masks(mask_table, pairs_here):
    pair_count = mask_table.shape[0]
    picker = (pairs_here[:, None] == jnp.arange(pair_count, dtype=jnp.int32)[None, :]).astype(
        jnp.bfloat16
    )
    flattened = mask_table.reshape(pair_count, -1).astype(jnp.bfloat16)
    looked = jnp.dot(picker, flattened, preferred_element_type=jnp.float32).astype(jnp.bfloat16)
    return looked.reshape(pairs_here.shape[0], mask_table.shape[1], mask_table.shape[2])


def masked_inputs(inputs, block_masks):
    row_count = inputs.shape[0]
    width = inputs.shape[1]
    blocks_in = block_masks.shape[2]
    blocks_out = block_masks.shape[0]
    pieces = inputs.reshape(row_count, blocks_in, width // blocks_in)
    masked = pieces[None, :, :, :] * block_masks[:, :, :, None]
    return masked.reshape(blocks_out, row_count, width)


def product_plain(inputs, weight, masks):
    columns = weight.shape[1]
    blocks_out = columns // BLOCK
    masked = masked_inputs(inputs, jnp.transpose(masks, (2, 0, 1)))
    weight_tiles = weight.reshape(weight.shape[0], blocks_out, BLOCK)
    result = jnp.einsum("nrk,knc->rnc", masked, weight_tiles, preferred_element_type=jnp.float32)
    return result.reshape(inputs.shape[0], columns)


def product_turned(inputs, weight, masks):
    columns = weight.shape[0]
    blocks_out = columns // BLOCK
    masked = masked_inputs(inputs, jnp.transpose(masks, (1, 0, 2)))
    weight_tiles = weight.reshape(blocks_out, BLOCK, weight.shape[1])
    result = jnp.einsum("nrk,nck->rnc", masked, weight_tiles, preferred_element_type=jnp.float32)
    return result.reshape(inputs.shape[0], columns)


def spread_rows(placer, values, groups, capacity):
    moved = jnp.dot(placer, values, preferred_element_type=jnp.float32).astype(jnp.bfloat16)
    return moved.reshape(groups, capacity, values.shape[1])


def route_grads(outgoing):
    return lax.all_to_all(outgoing, "dp", split_axis=0, concat_axis=0, tiled=True)


def widen(pieces):
    return jax.tree.map(
        lambda part, own: part.astype(own.dtype),
        lax.all_gather(as_sent(pieces), "tensor", axis=1, tiled=True),
        pieces,
    )


def settle(pieces):
    return jax.tree.map(
        lambda part: part.astype(jnp.float32),
        lax.psum_scatter(as_sent(pieces), "tensor", scatter_dimension=1, tiled=True),
    )


def send_back(values, placer, groups, capacity):
    returned = lax.all_to_all(
        values.reshape(groups, capacity, values.shape[1]),
        "dp",
        split_axis=0,
        concat_axis=0,
        tiled=True,
    )
    flattened = returned.reshape(groups * capacity, values.shape[1])
    return jnp.dot(placer.T, flattened, preferred_element_type=jnp.float32).astype(jnp.bfloat16)


def per_device(tokens, cotangent, pair_ids, up_mask, down_mask, up_weight, down_weight):
    groups = lax.axis_size("dp")
    tok_count = pair_ids.shape[0]
    capacity = max(2, (3 * tok_count + 2 * groups - 1) // (2 * groups))
    slot_count = groups * capacity
    target = pair_ids % groups
    matches = (target[:, None] == jnp.arange(groups, dtype=jnp.int32)[None, :]).astype(jnp.int32)
    before = jnp.sum((jnp.cumsum(matches, axis=0) - matches) * matches, axis=1)
    position = target * capacity + before
    placing = position[None, :] == jnp.arange(slot_count, dtype=jnp.int32)[:, None]
    placer = placing.astype(jnp.bfloat16)
    slot_pairs = jnp.sum(jnp.where(placing, pair_ids[None, :] + 1, 0), axis=1) - 1
    outgoing = spread_rows(placer, tokens, groups, capacity)
    arrived, arrived_pairs = (
        lax.all_to_all(outgoing, "dp", split_axis=0, concat_axis=0, tiled=True),
        lax.all_to_all(
            slot_pairs.reshape(groups, capacity), "dp", split_axis=0, concat_axis=0, tiled=True
        ),
    )
    pairs_here = arrived_pairs.reshape(-1)
    up_rows = row_masks(up_mask, pairs_here)
    down_rows = row_masks(down_mask, pairs_here)
    down_local = down_weight[0]
    grads_out = spread_rows(placer, cotangent, groups, capacity)
    (gathered,) = widen((arrived.reshape(slot_count, -1),))
    before_act = product_plain(gathered, up_weight, up_rows)
    activated, backward_function = jax.vjp(jax.nn.gelu, before_act)
    hidden = activated.astype(jnp.bfloat16)
    blended_portion, backward_function = (
        product_plain(hidden, down_local, down_rows).astype(jnp.bfloat16),
        backward_function,
    )
    (mixed_sum,) = settle((blended_portion,))
    arrived_grads = route_grads(grads_out)
    (grad_rows,) = widen((arrived_grads.reshape(slot_count, -1),))
    grad_hidden = product_turned(grad_rows, down_local, down_rows)
    grad_pre = backward_function(grad_hidden)[0].astype(jnp.bfloat16)
    input_part = product_turned(grad_pre, up_weight, up_rows).astype(jnp.bfloat16)
    (input_sum,) = settle((input_part,))
    mixed = send_back(mixed_sum.astype(jnp.bfloat16), placer, groups, capacity)
    token_grads = send_back(input_sum.astype(jnp.bfloat16), placer, groups, capacity)
    return (mixed, token_grads)


def solution(mesh):
    return jax.shard_map(
        per_device,
        mesh=mesh,
        in_specs=(
            P("dp", "tensor"),
            P("dp", "tensor"),
            P("dp"),
            P(None, None, "tensor"),
            P(None, "tensor", None),
            P(None, "tensor"),
            P("dp", "tensor", None),
        ),
        out_specs=(P("dp", "tensor"), P("dp", "tensor")),
        check_vma=False,
    )
```

profile of v0, /device:TPU:0, one launch (start us, length us, event | category | flops | bytes accessed | tf_op | source)
XLA Modules:
  0.0 283.2 jit_solution(5968188112423936378)
XLA Ops:
  7.2 0.7 and_select_fusion
  8.0 0.2 reduce_window_sum.11
  8.1 0.2 select_reduce_fusion.1
  8.3 0.1 select_reduce_fusion
  8.5 0.7 sub.16
  9.1 7.3 %all-to-all-start.1 = ((s32[8,1,24]{2,1,0:T(1,128)}), s32[8,1,24]{2,1,0:T(1,128)S(1)}, u32[]{:S(2)}, u32[]{:S(2)}) async-start(s32[8,1,24]{2,1,0:T(1,128)} %sub.16), calls=%async_computation.1 | async-start | bytes 8192 | tf_op jit(solution)/shard_map/all_to_all | solution.py:106
  16.4 0.9 convolution_convert_fusion.1
  17.3 5.5 %all-to-all-done.1 = s32[8,1,24]{2,1,0:T(1,128)S(1)} async-done(((s32[8,1,24]{2,1,0:T(1,128)}), s32[8,1,24]{2,1,0:T(1,128)S(1)}, u32[]{:S(2)}, u32[]{:S(2)}) %all-to-all-start.1) | async-done | bytes 800 | tf_op jit(solution)/shard_map/all_to_all | solution.py:106
  22.8 3.4 %all-to-all-start = ((bf16[8,24,512]{2,1,0:T(8,128)(2,1)}), bf16[8,24,512]{2,1,0:T(8,128)(2,1)S(1)}, u32[]{:S(2)}, u32[]{:S(2)}) async-start(bf16[8,24,512]{2,1,0:T(8,128)(2,1)} %bitcast), calls=%async_computation | async-start | bytes 393216 | tf_op jit(solution)/shard_map/all_to_all | solution.py:105
  26.2 1.8 convolution_convert_fusion
  28.0 0.9 convert_element_type.70
  28.9 0.9 convert_element_type.74
  29.8 9.8 %copy.44 = bf16[256,8,16,128]{3,2,1,0:T(8,128)(2,1)} copy(bf16[256,8,16,128]{3,1,2,0:T(8,128)(2,1)} %bitcast.103) | data formatting | bytes 16777216
  39.6 0.5 broadcast.104
  40.1 0.7 reduce.3
  40.9 0.2 convolution_convert_fusion.5
  41.1 5.9 %all-to-all-start.3 = ((bf16[8,24,512]{2,1,0:T(8,128)(2,1)}), bf16[8,24,512]{2,1,0:T(8,128)(2,1)S(1)}, u32[]{:S(2)}, u32[]{:S(2)}) async-start(bf16[8,24,512]{2,1,0:T(8,128)(2,1)} %bitcast.12), calls=%async_computation.4 | async-start | bytes 393216 | tf_op jit(solution)/shard_map/all_to_all | solution.py:61
  47.1 0.2 convolution_convert_fusion.4
  47.4 0.4 copy.28
  47.8 8.5 %mul.154 = bf16[16,192,16,128]{3,2,1,0:T(8,128)(2,1)} broadcast(bf16[16,192,16]{2,1,0:T(8,128)(2,1)S(1)} %copy.28), dimensions={0,1,2} | broadcast | bytes 12681216 | tf_op jit(solution)/shard_map/mul | solution.py:33
  56.3 19.3 %mul.155 = bf16[16,192,2048]{2,1,0:T(8,128)(2,1)} reshape(bf16[16,192,16,128]{3,2,1,0:T(8,128)(2,1)} %mul.154) | data formatting | bytes 25165824 | tf_op jit(solution)/shard_map/mul | solution.py:33
  75.7 0.4 copy.35
  76.1 8.5 %mul.167 = bf16[16,192,16,128]{3,2,1,0:T(8,128)(2,1)} broadcast(bf16[16,192,16]{2,1,0:T(8,128)(2,1)S(1)} %copy.35), dimensions={0,1,2} | broadcast | bytes 12681216 | tf_op jit(solution)/shard_map/mul | solution.py:33
  84.6 19.3 %mul.168 = bf16[16,192,2048]{2,1,0:T(8,128)(2,1)} reshape(bf16[16,192,16,128]{3,2,1,0:T(8,128)(2,1)} %mul.167) | data formatting | bytes 25165824 | tf_op jit(solution)/shard_map/mul | solution.py:33
  103.9 0.4 copy.37
  104.3 8.5 %mul.183 = bf16[16,192,16,128]{3,2,1,0:T(8,128)(2,1)} broadcast(bf16[16,192,16]{2,1,0:T(8,128)(2,1)S(1)} %copy.37), dimensions={0,1,2} | broadcast | bytes 12681216 | tf_op jit(solution)/shard_map/mul | solution.py:33
  112.8 19.3 %mul.184 = bf16[16,192,2048]{2,1,0:T(8,128)(2,1)} reshape(bf16[16,192,16,128]{3,2,1,0:T(8,128)(2,1)} %mul.183) | data formatting | bytes 25165824 | tf_op jit(solution)/shard_map/mul | solution.py:33
  132.1 0.4 copy.32
  132.5 8.5 %mul.163 = bf16[16,192,16,128]{3,2,1,0:T(8,128)(2,1)} broadcast(bf16[16,192,16]{2,1,0:T(8,128)(2,1)S(1)} %copy.32), dimensions={0,1,2} | broadcast | bytes 12681216 | tf_op jit(solution)/shard_map/mul | solution.py:33
  141.0 19.3 %mul.164 = bf16[16,192,2048]{2,1,0:T(8,128)(2,1)} reshape(bf16[16,192,16,128]{3,2,1,0:T(8,128)(2,1)} %mul.163) | data formatting | bytes 25165824 | tf_op jit(solution)/shard_map/mul | solution.py:33
  160.3 8.6 %all_gather.6 = bf16[192,2048]{1,0:T(8,128)(2,1)S(1)} all-gather(bf16[192,512]{1,0:T(8,128)(2,1)S(1)} %bitcast.115), channel_id=1, replica_groups=mesh['dp'=8,'tensor'=4] {'tensor'}, dimensions={1}, use_global_device_ids=true | all-gather | bytes 983040 | tf_op jit(solution)/shard_map/all_gather | solution.py:67
  168.9 8.9 %all_gather.7 = bf16[192,2048]{1,0:T(8,128)(2,1)S(1)} all-gather(bf16[192,512]{1,0:T(8,128)(2,1)S(1)} %bitcast.116), channel_id=1, replica_groups=mesh['dp'=8,'tensor'=4] {'tensor'}, dimensions={1}, use_global_device_ids=true | all-gather | bytes 983040 | tf_op jit(solution)/shard_map/all_gather | solution.py:67
  177.8 10.6 %fusion.6 = f32[16,192,128]{2,1,0:T(8,128)S(1)} fusion(bf16[16,192,2048]{2,1,0:T(8,128)(2,1)} %mul.155, bf16[192,2048]{1,0:T(8,128)(2,1)S(1)} %all_gather.6, bf16[2048,2048]{1,0:T(8,128)(2,1)} %param.12), kind=kOutput, calls=%fused_computation.6 | convolution fusion | flops 1616904192 | bytes 23330816 | tf_op jit(solution)/shard_map/nrk,knc->rnc/dot_general | solution.py:42
  188.4 0.5 copy_bitcast_fusion.3
  188.9 11.1 %fusion.44 = bf16[16,24,8,128]{3,2,1,0:T(8,128)(2,1)S(1)} fusion(f32[16,192,128]{2,1,0:T(8,128)S(1)} %fusion.6, bf16[16,128,2048]{2,1,0:T(8,128)(2,1)} %bitcast.104, bf16[16,192,2048]{2,1,0:T(8,128)(2,1)} %mul.168, bf16[192,2048]{1,0:T(8,128)(2,1)S(1)} %all_gather.7), kind=kOutput, calls=%fused_computation.41 | convolution fusion | flops 1624768512 | bytes 24117248 | tf_op jit(solution)/shard_map/nrk,nck->rnc/dot_general | solution.py:51
  200.0 0.2 copy.60
  200.2 10.8 %fusion.34 = bf16[16,24,8,128]{3,2,1,0:T(8,128)(2,1)S(1)} fusion(bf16[16,128,2048]{2,1,0:T(8,128)(2,1)} %bitcast.121, bf16[16,192,2048]{2,1,0:T(8,128)(2,1)} %mul.184, bf16[192,2048]{1,0:T(8,128)(2,1)S(1)} %bitcast.112), kind=kOutput, calls=%fused_computation.33 | convolution fusion | flops 1617297408 | bytes 22544384 | tf_op jit(solution)/shard_map/nrk,nck->rnc/dot_general | solution.py:51
  211.0 1.1 copy.59
  212.1 0.3 reduce-scatter.3.cloned.1.call-start
  212.4 13.6 %fusion.37 = bf16[16,24,8,128]{3,2,1,0:T(8,128)(2,1)S(1)} fusion(bf16[2048,16,128]{2,1,0:T(8,128)(2,1)} %bitcast.105, bf16[16,192,2048]{2,1,0:T(8,128)(2,1)} %mul.164, bf16[192,2048]{1,0:T(8,128)(2,1)S(1)} %copy_bitcast_fusion.3), kind=kOutput, calls=%fused_computation.34 | convolution fusion | flops 1617297408 | bytes 22544384 | tf_op jit(solution)/shard_map/nrk,knc->rnc/dot_general | solution.py:42
  226.0 1.1 copy.61
  227.1 8.9 %reduce-scatter.5.cloned.1.call-done = bf16[192,512]{1,0:T(8,128)(2,1)} async-done(((bf16[192,2048]{1,0:T(8,128)(2,1)}), bf16[192,512]{1,0:T(8,128)(2,1)}) %reduce-scatter.5.cloned.1.call-update) | async-done | bytes 196624 | tf_op jit(solution)/shard_map/reduce_scatter | solution.py:75
  236.0 5.5 %all-to-all-start.4 = ((bf16[8,24,512]{2,1,0:T(8,128)(2,1)}), bf16[8,24,512]{2,1,0:T(8,128)(2,1)S(1)}, u32[]{:S(2)}, u32[]{:S(2)}) async-start(bf16[8,24,512]{2,1,0:T(8,128)(2,1)} %bitcast.119), calls=%async_computation.6 | async-start | bytes 393216 | tf_op jit(solution)/shard_map/all_to_all | solution.py:80
  241.5 20.5 %reduce-scatter.3.cloned.1.call-done = bf16[192,512]{1,0:T(8,128)(2,1)} async-done(((bf16[192,2048]{1,0:T(8,128)(2,1)}), bf16[192,512]{1,0:T(8,128)(2,1)}) %reduce-scatter.3.cloned.1.call-update) | async-done | bytes 196624 | tf_op jit(solution)/shard_map/reduce_scatter | solution.py:75
  262.0 5.5 %all-to-all-start.2 = ((bf16[8,24,512]{2,1,0:T(8,128)(2,1)}), bf16[8,24,512]{2,1,0:T(8,128)(2,1)S(1)}, u32[]{:S(2)}, u32[]{:S(2)}) async-start(bf16[8,24,512]{2,1,0:T(8,128)(2,1)} %bitcast.120), calls=%async_computation.3 | async-start | bytes 393216 | tf_op jit(solution)/shard_map/all_to_all | solution.py:80
  267.5 0.9 convolution_convert_fusion.2
  268.4 7.1 %all-to-all-done.2 = bf16[8,24,512]{2,1,0:T(8,128)(2,1)S(1)} async-done(((bf16[8,24,512]{2,1,0:T(8,128)(2,1)}), bf16[8,24,512]{2,1,0:T(8,128)(2,1)S(1)}, u32[]{:S(2)}, u32[]{:S(2)}) %all-to-all-start.2) | async-done | bytes 196640 | tf_op jit(solution)/shard_map/all_to_all | solution.py:80
  275.5 0.9 convolution_convert_fusion.3
  (16 shorter events, 0.5 us)
Async XLA Ops:
  7.2 9.3 %copy-start = (bf16[128,512]{1,0:T(8,128)(2,1)S(1)}, bf16[128,512]{1,0:T(8,128)(2,1)}, u32[]{:S(2)}) copy-start(bf16[128,512]{1,0:T(8,128)(2,1)} %param.7) | copy-start | bytes 393220
  9.1 13.7 %all-to-all-start.1 = ((s32[8,1,24]{2,1,0:T(1,128)}), s32[8,1,24]{2,1,0:T(1,128)S(1)}, u32[]{:S(2)}, u32[]{:S(2)}) async-start(s32[8,1,24]{2,1,0:T(1,128)} %sub.16), calls=%async_computation.1 | async-start | bytes 8192 | tf_op jit(solution)/shard_map/all_to_all | solution.py:106
  22.8 18.3 %all-to-all-start = ((bf16[8,24,512]{2,1,0:T(8,128)(2,1)}), bf16[8,24,512]{2,1,0:T(8,128)(2,1)S(1)}, u32[]{:S(2)}, u32[]{:S(2)}) async-start(bf16[8,24,512]{2,1,0:T(8,128)(2,1)} %bitcast), calls=%async_computation | async-start | bytes 393216 | tf_op jit(solution)/shard_map/all_to_all | solution.py:105
  41.1 127.8 %all-to-all-start.3 = ((bf16[8,24,512]{2,1,0:T(8,128)(2,1)}), bf16[8,24,512]{2,1,0:T(8,128)(2,1)S(1)}, u32[]{:S(2)}, u32[]{:S(2)}) async-start(bf16[8,24,512]{2,1,0:T(8,128)(2,1)} %bitcast.12), calls=%async_computation.4 | async-start | bytes 393216 | tf_op jit(solution)/shard_map/all_to_all | solution.py:61
  47.0 189.0 %reduce-scatter.5.cloned.1.call-start = ((), (), s32[]{:S(2)}) async-start(), calls=%async_computation.8 | async-start | bytes 983040 | tf_op jit(solution)/shard_map/reduce_scatter | solution.py:75
  212.1 49.9 %reduce-scatter.3.cloned.1.call-start = ((), (), s32[]{:S(2)}) async-start(), calls=%async_computation.7 | async-start | bytes 983040 | tf_op jit(solution)/shard_map/reduce_scatter | solution.py:75
  212.4 64.0 %copy-start.1 = (bf16[128,512]{1,0:T(8,128)(2,1)S(1)}, bf16[128,512]{1,0:T(8,128)(2,1)}, u32[]{:S(2)}) copy-start(bf16[128,512]{1,0:T(8,128)(2,1)} %param.7) | copy-start | bytes 393220
  236.0 26.0 %all-to-all-start.4 = ((bf16[8,24,512]{2,1,0:T(8,128)(2,1)}), bf16[8,24,512]{2,1,0:T(8,128)(2,1)S(1)}, u32[]{:S(2)}, u32[]{:S(2)}) async-start(bf16[8,24,512]{2,1,0:T(8,128)(2,1)} %bitcast.119), calls=%async_computation.6 | async-start | bytes 393216 | tf_op jit(solution)/shard_map/all_to_all | solution.py:80
  262.0 13.5 %all-to-all-start.2 = ((bf16[8,24,512]{2,1,0:T(8,128)(2,1)}), bf16[8,24,512]{2,1,0:T(8,128)(2,1)S(1)}, u32[]{:S(2)}, u32[]{:S(2)}) async-start(bf16[8,24,512]{2,1,0:T(8,128)(2,1)} %bitcast.120), calls=%async_computation.3 | async-start | bytes 393216 | tf_op jit(solution)/shard_map/all_to_all | solution.py:80
Sparse Core Ops, SparseCore 0:
  212.2 23.7 reduce-scatter.4
  238.7 23.2 reduce-scatter.2
where the time goes:
time: 286 us; the launch traced here: 283 us
  local copies, waits for them, and re-layouts  126 us (44%)
  matrix products  50.9 us (18%)
  waiting for transfers between devices  42 us (15%)
  starting transfers between devices  28 us (10%)
  blocking collectives  17.5 us (6%)
  between operations  14.2 us (5%)
  other arithmetic  4.24 us (1%)
    mul x9, local copies, waits for them, and re-layouts, masked_inputs(): masked = pieces[None, :, :, :] * block_masks[:, :, :, None]  111 us
    reduce_scatter x2, waiting for transfers between devices, settle(): lax.psum_scatter(as_sent(pieces), 'tensor', scatter_dimension=1, tiled=True)  29.4 us
    dot_general x2, matrix products, product_plain(): jnp.einsum('nrk,knc->rnc', masked, weight_tiles, preferred_element_type=j...  24.2 us
    dot_general x2, matrix products, product_turned(): jnp.einsum('nrk,nck->rnc', masked, weight_tiles, preferred_element_type=j...  21.9 us
    all_gather x2, blocking collectives, widen(): lax.all_gather(as_sent(pieces), 'tensor', axis=1, tiled=True)  17.5 us
    all_to_all x2, starting transfers between devices, send_back(): lax.all_to_all(values.reshape(groups, capacity, values.shape[1]), 'dp', s...  11 us
    unnamed x5, local copies, waits for them, and re-layouts  9.79 us
    all_to_all x1, starting transfers between devices, per_device(): lax.all_to_all(slot_pairs.reshape(groups, capacity), 'dp', split_axis=0,...  7.28 us
  transfers between devices with their start and end apart: 7, of which 4 were waited for; matrix products, arithmetic and copies ran while one was open for 51% of the time, Pallas kernels for 0%

commit v1 on v0

v1 whole, which is shorter than its diff:
```python
import functools

import jax
import jax.numpy as jnp
from jax import lax
from jax.experimental import pallas as pl
from jax.experimental.pallas import tpu as pltpu
from jax.sharding import PartitionSpec as P

BLOCK = 128
ROOT = 0.7978845608028654
CUBE = 0.044715
NT = (((1,), (1,)), ((), ()))
NN = (((1,), (0,)), ((), ()))


def dot(a, b, dims=NN):
    return lax.dot_general(a, b, dims, preferred_element_type=jnp.float32)


def gelu_pair(v):
    square = v * v
    t = jnp.tanh(ROOT * (v + CUBE * v * square))
    half = 0.5 * (1.0 + t)
    slope = half + 0.5 * v * (1.0 - t * t) * (ROOT * (1.0 + 3.0 * CUBE * square))
    return v * half, slope


def masked(values_ref, bits, blocks):
    rows = values_ref.shape[0]
    parts = []
    for b in range(blocks):
        own = jnp.broadcast_to(bits[:, b : b + 1], (rows, BLOCK))
        parts.append(values_ref[:, b * BLOCK : (b + 1) * BLOCK] * own)
    return jnp.concatenate(parts, axis=1)


def products(x_ref, g_ref, pick, up_ref, down_ref, wu_ref, wd_ref, h_ref, q_ref, mixed_ref, input_ref):
    blocks_d, blocks_f = up_ref.shape[0], up_ref.shape[1]

    def first(f, _):
        at = pl.ds(pl.multiple_of(f * BLOCK, BLOCK), BLOCK)
        up_bits = dot(pick, up_ref[:, f, :].astype(jnp.bfloat16), NT).astype(jnp.bfloat16)
        down_bits = dot(pick, down_ref[f].astype(jnp.bfloat16), NT).astype(jnp.bfloat16)
        pre = dot(masked(x_ref, up_bits, blocks_d), wu_ref[:, at])
        grad = dot(masked(g_ref, down_bits, blocks_d), wd_ref[at, :], NT)
        act, slope = gelu_pair(pre)
        h_ref[:, at] = act.astype(jnp.bfloat16)
        q_ref[:, at] = (grad * slope).astype(jnp.bfloat16)
        return 0

    def second(d, _):
        at = pl.ds(pl.multiple_of(d * BLOCK, BLOCK), BLOCK)
        up_bits = dot(pick, up_ref[d].astype(jnp.bfloat16), NT).astype(jnp.bfloat16)
        down_bits = dot(pick, down_ref[:, d, :].astype(jnp.bfloat16), NT).astype(jnp.bfloat16)
        mixed_ref[:, at] = dot(masked(h_ref, down_bits, blocks_f), wd_ref[:, at]).astype(jnp.bfloat16)
        input_ref[:, at] = dot(masked(q_ref, up_bits, blocks_f), wu_ref[at, :], NT).astype(jnp.bfloat16)
        return 0

    lax.fori_loop(0, blocks_f, first, 0)
    lax.fori_loop(0, blocks_d, second, 0)


def compute_kernel(x_ref, g_ref, pick_ref, up_ref, down_ref, wu_hbm, wd_hbm, mixed_ref, input_ref,
                   wu_ref, wd_ref, h_ref, q_ref, sems):
    load_up = pltpu.make_async_copy(wu_hbm, wu_ref, sems.at[0])
    load_down = pltpu.make_async_copy(wd_hbm, wd_ref, sems.at[1])
    load_up.start()
    load_down.start()
    load_up.wait()
    load_down.wait()
    products(x_ref, g_ref, pick_ref[...], up_ref, down_ref, wu_ref, wd_ref, h_ref, q_ref, mixed_ref, input_ref)


def compute(x, g, pick, up_table, down_table, up_weight, down_weight):
    rows, width = x.shape
    hidden = up_weight.shape[1]
    vmem = pl.BlockSpec(memory_space=pltpu.VMEM)
    anywhere = pl.BlockSpec(memory_space=pl.ANY)
    return pl.pallas_call(
        compute_kernel,
        out_shape=[jax.ShapeDtypeStruct((rows, width), jnp.bfloat16)] * 2,
        in_specs=[vmem] * 5 + [anywhere] * 2,
        out_specs=[vmem] * 2,
        scratch_shapes=[
            pltpu.VMEM(up_weight.shape, jnp.bfloat16),
            pltpu.VMEM(down_weight.shape, jnp.bfloat16),
            pltpu.VMEM((rows, hidden), jnp.bfloat16),
            pltpu.VMEM((rows, hidden), jnp.bfloat16),
            pltpu.SemaphoreType.DMA((2,)),
        ],
        compiler_params=pltpu.CompilerParams(vmem_limit_bytes=44 * 2**20),
        name="masked_products",
    )(x, g, pick, up_table, down_table, up_weight, down_weight)


def place(pair_ids, groups, capacity):
    target = pair_ids % groups
    matches = (target[:, None] == jnp.arange(groups, dtype=jnp.int32)[None, :]).astype(jnp.int32)
    before = jnp.sum((jnp.cumsum(matches, axis=0) - matches) * matches, axis=1)
    position = target * capacity + before
    slots = jnp.arange(groups * capacity, dtype=jnp.int32)
    return (position[None, :] == slots[:, None]).astype(jnp.bfloat16)


def swap(values, groups, capacity):
    width = values.shape[1]
    moved = lax.all_to_all(
        values.reshape(groups, capacity, width), "dp", split_axis=0, concat_axis=0, tiled=True
    )
    return moved.reshape(groups * capacity, width)


def per_device(tokens, cotangent, pair_ids, up_mask, down_mask, up_weight, down_weight):
    groups = lax.axis_size("dp")
    tok_count, part = tokens.shape
    pairs = up_mask.shape[0]
    capacity = max(2, (3 * tok_count + 2 * groups - 1) // (2 * groups))
    slot_count = groups * capacity
    placer = place(pair_ids, groups, capacity)
    lanes = -(-pairs // BLOCK) * BLOCK
    known = (pair_ids[:, None] == jnp.arange(lanes, dtype=jnp.int32)[None, :]).astype(jnp.bfloat16)
    pad = ((0, 0), (0, 0), (0, lanes - pairs))
    up_table = jnp.pad(jnp.transpose(up_mask, (1, 2, 0)), pad)
    down_table = jnp.pad(jnp.transpose(down_mask, (1, 2, 0)), pad)

    leaving = jnp.concatenate([tokens, cotangent, known], axis=1)
    moved = swap(dot(placer, leaving).astype(jnp.bfloat16), groups, capacity)
    both = jnp.stack([moved[:, :part], moved[:, part : 2 * part]])
    whole = lax.all_gather(both, "tensor", axis=2, tiled=True)
    mixed_part, input_part = compute(
        whole[0], whole[1], moved[:, 2 * part :], up_table, down_table, up_weight, down_weight[0]
    )
    summed = lax.psum_scatter(
        jnp.stack([mixed_part, input_part]), "tensor", scatter_dimension=2, tiled=True
    )
    back = swap(jnp.concatenate([summed[0], summed[1]], axis=1), groups, capacity)
    out = lax.dot_general(
        placer, back, (((0,), (0,)), ((), ())), preferred_element_type=jnp.float32
    ).astype(jnp.bfloat16)
    return out[:, :part], out[:, part:]


def solution(mesh):
    return jax.shard_map(
        per_device,
        mesh=mesh,
        in_specs=(
            P("dp", "tensor"),
            P("dp", "tensor"),
            P("dp"),
            P(None, None, "tensor"),
            P(None, "tensor", None),
            P(None, "tensor"),
            P("dp", "tensor", None),
        ),
        out_specs=(P("dp", "tensor"), P("dp", "tensor")),
        check_vma=False,
    )
```

time: 286 us -> 146 us (0.51)
  local copies, waits for them, and re-layouts: 126 us -> 3.37 us
  matrix products: 50.9 us -> 1.5 us
  Pallas kernels: 0 us -> 37.5 us
  starting transfers between devices: 28 us -> 0.08 us
  blocking collectives: 17.5 us -> 37.6 us
  waiting for transfers between devices: 42 us -> 46.9 us
    mul x9 -> x0, local copies, waits for them, and re-layouts: 111 us -> none  [masked_inputs(): masked = pieces[None, :, :, :] * block_masks[:, :, :, None]]
    dot_general x10 -> x2, matrix products: 50.9 us -> 1.5 us  [the longest x1 1.23 us: dot(): return lax.dot_general(a, b, dims, preferred_element_type=jnp.float32)]
    all_to_all x0 -> x2, blocking collectives: none -> 37.6 us  [swap(): lax.all_to_all(values.reshape(groups, capacity, width), 'dp', split_axis=...]
    pallas_call x0 -> x1, Pallas kernels: none -> 37.5 us  [compute(): pl.pallas_call(compute_kernel, out_shape=[jax.ShapeDtypeStruct((rows, wid...]
    all_to_all x5 -> x0, starting transfers between devices: 27.7 us -> none  [the longest x2 11 us: send_back(): lax.all_to_all(values.reshape(groups, capacity, values.shape[1]), 'dp', s...]
    all_gather x0 -> x1, waiting for transfers between devices: none -> 18.5 us  [per_device(): whole = lax.all_gather(both, 'tensor', axis=2, tiled=True)]
    all_gather x2 -> x0, blocking collectives: 17.5 us -> none  [widen(): lax.all_gather(as_sent(pieces), 'tensor', axis=1, tiled=True)]
    all_to_all x5 -> x0, waiting for transfers between devices: 12.6 us -> none  [the longest x2 7.08 us: send_back(): lax.all_to_all(values.reshape(groups, capacity, values.shape[1]), 'dp', s...]
  transfers between devices with their start and end apart: 7 -> 2, of which waited for: 4 -> 2; matrix products, arithmetic and copies ran while one was open for 51% -> 0% of each run, Pallas kernels for 0% -> 0%
where the time goes in v1:
time: 146 us
  waiting for transfers between devices  46.9 us (32%)
  blocking collectives  37.6 us (26%)
  Pallas kernels  37.5 us (26%)
  between operations  14.2 us (10%)
  other arithmetic  4.62 us (3%)
  local copies, waits for them, and re-layouts  3.37 us (2%)
  matrix products  1.5 us (1%)
    all_to_all x2, blocking collectives, swap(): lax.all_to_all(values.reshape(groups, capacity, width), 'dp', split_axis=...  37.6 us
    pallas_call x1, Pallas kernels, compute(): pl.pallas_call(compute_kernel, out_shape=[jax.ShapeDtypeStruct((rows, wid...  37.5 us
    reduce_scatter x1, waiting for transfers between devices, per_device(): lax.psum_scatter(jnp.stack([mixed_part, input_part]), 'tensor', scatter_d...  28.3 us
    all_gather x1, waiting for transfers between devices, per_device(): whole = lax.all_gather(both, 'tensor', axis=2, tiled=True)  18.5 us
  transfers between devices with their start and end apart: 2, of which 2 were waited for; matrix products, arithmetic and copies ran while one was open for 0% of the time, Pallas kernels for 0%

profile of v1, /device:TPU:0, one launch (start us, length us, event | category | flops | bytes accessed | tf_op | source)
XLA Modules:
  0.0 145.6 jit_solution(4158831142266578526)
XLA Ops:
  7.2 0.0 all-gather.2.cloned.1.call-start
  7.2 0.7 and_select_fusion
  7.9 0.7 fusion.6
  8.6 0.1 fusion.5
  8.7 0.2 reduce_window_sum.11
  8.9 0.2 select_reduce_fusion
  9.1 0.7 multiply_add_fusion
  9.7 1.2 convolution_convert_fusion
  11.0 0.0 copy-start
  11.0 0.0 copy-start.1
  11.0 20.2 %all_to_all.10 = bf16[8,24,1152]{2,1,0:T(8,128)(2,1)S(1)} all-to-all(bf16[8,24,1152]{2,1,0:T(8,128)(2,1)S(1)} %bitcast.27), channel_id=1, replica_groups=mesh['dp'=8,'tensor'=4] {'dp'}, dimensions={0} | all-to-all | bytes 884736 | tf_op jit(solution)/shard_map/all_to_all | solution.py:108
  31.2 0.8 pad_maximum_fusion.1
  32.0 0.0 all-gather.2.cloned.1.call-update
  32.0 0.0 reduce-scatter.2.cloned.1.call-start
  32.0 0.0 copy-done
  32.1 0.0 copy-done.1
  32.1 18.5 %all-gather.2.cloned.1.call-done = bf16[2,192,2048]{2,1,0:T(8,128)(2,1)} async-done(((bf16[2,192,512]{2,1,0:T(8,128)(2,1)}), bf16[2,192,2048]{2,1,0:T(8,128)(2,1)}) %all-gather.2.cloned.1.call-update) | async-done | bytes 1572880 | tf_op jit(solution)/shard_map/all_gather | solution.py:130
  50.6 1.5 %slice_bitcast_fusion = (bf16[192,2048]{1,0:T(8,128)(2,1)S(1)}, bf16[192,2048]{1,0:T(8,128)(2,1)S(1)}) fusion(bf16[2,192,2048]{2,1,0:T(8,128)(2,1)} %all-gather.2.cloned.1.call-done), kind=kLoop, calls=%fused_computation.3 | loop fusion | bytes 3145728 | tf_op jit(solution)/shard_map/squeeze | solution.py:132
  52.2 37.5 %masked_products.1 = (bf16[192,2048]{1,0:T(8,128)(2,1)S(1)}, bf16[192,2048]{1,0:T(8,128)(2,1)S(1)}) custom-call(bf16[192,2048]{1,0:T(8,128)(2,1)S(1)} %get-tuple-element.7.x_ref, bf16[192,2048]{1,0:T(8,128)(2,1)S(1)} %get-tuple-element.6.g_ref, bf16[192,128]{1,0:T(8,128)(2,1)S(1)} %slice.40.pick_ref, s32[16,16,128]{2,1,0:T(8,128)S(1)} %pad.7.up_ref, ...), custom_call_target="tpu_custom_call" | custom-call | tf_op jit(solution)/shard_map/masked_products/pallas_call | solution.py:80
  89.7 1.3 pad_maximum_fusion
  91.0 0.0 reduce-scatter.2.cloned.1.call-update
  91.0 28.3 %reduce-scatter.2.cloned.1.call-done = bf16[2,192,512]{2,1,0:T(8,128)(2,1)} async-done(((bf16[2,192,2048]{2,1,0:T(8,128)(2,1)}), bf16[2,192,512]{2,1,0:T(8,128)(2,1)}) %reduce-scatter.2.cloned.1.call-update) | async-done | bytes 393232 | tf_op jit(solution)/shard_map/reduce_scatter | solution.py:134
  119.3 1.0 fusion.11
  120.4 17.4 %all_to_all.11 = bf16[8,24,1024]{2,1,0:T(8,128)(2,1)S(1)} all-to-all(bf16[8,24,1024]{2,1,0:T(8,128)(2,1)S(1)} %pad_maximum_fusion.2), channel_id=1, replica_groups=mesh['dp'=8,'tensor'=4] {'dp'}, dimensions={0} | all-to-all | bytes 786432 | tf_op jit(solution)/shard_map/all_to_all | solution.py:108
  137.8 0.3 convolution_convert_fusion.1
  138.1 0.7 fusion.12
  (5 shorter events, 0.1 us)
Async XLA Ops:
  7.2 43.5 %all-gather.2.cloned.1.call-start = ((), (), s32[]{:S(2)}) async-start(), calls=%async_computation.3 | async-start | bytes 1966080 | tf_op jit(solution)/shard_map/all_gather | solution.py:130
  11.0 21.1 %copy-start = (s32[100,16,16]{0,2,1:T(8,128)S(1)}, s32[100,16,16]{0,2,1:T(8,128)}, u32[]{:S(2)}) copy-start(s32[100,16,16]{0,2,1:T(8,128)} %param.10) | copy-start | bytes 307204
  11.0 21.1 %copy-start.1 = (s32[100,16,16]{0,2,1:T(8,128)S(1)}, s32[100,16,16]{0,2,1:T(8,128)}, u32[]{:S(2)}) copy-start(s32[100,16,16]{0,2,1:T(8,128)} %param.11) | copy-start | bytes 307204
  32.0 87.3 %reduce-scatter.2.cloned.1.call-start = ((), (), s32[]{:S(2)}) async-start(), calls=%async_computation.4 | async-start | bytes 1966080 | tf_op jit(solution)/shard_map/reduce_scatter | solution.py:134
Sparse Core Ops, SparseCore 0:
  32.1 18.4 all-gather.1
  91.1 28.1 reduce-scatter.1

commit v2 on v1

--- a/solution.py
+++ b/solution.py
@@ -94,6 +94,324 @@
     )(x, g, pick, up_table, down_table, up_weight, down_weight)
 
 
+MESH = pl.DeviceIdType.MESH
+
+
+def stacked(values, row, count):
+    wide = values.shape[1] // BLOCK
+    return jnp.concatenate(
+        [values[row : row + count, b * BLOCK : (b + 1) * BLOCK] for b in range(wide)], axis=0
+    ).astype(jnp.bfloat16)
+
+
+def unstack(slab, into_ref, row, column, count):
+    wide = slab.astype(jnp.float32)
+    for b in range(slab.shape[0] // count):
+        into_ref[row : row + count, column + b * BLOCK : column + (b + 1) * BLOCK] = wide[
+            b * count : (b + 1) * count
+        ]
+
+
+def layer_kernel(groups, capacity, tokens_ref, cotangent_ref, pairs_ref, up_ref, down_ref, wu_hbm, wd_hbm,
+                 mixed_ref, grads_ref,
+                 wu_ref, wd_ref, eu_ref, ed_ref, send_p, send_a, send_b, got_p, got_a, got_b,
+                 wide_ref, x_ref, g_ref, h_ref, q_ref, slope_ref,
+                 part_m, part_i, sib_m, sib_i, out_m, out_i, in_m, in_i,
+                 back_m, back_i, home_m, home_i, local_sems, ss, rs):
+    slots = groups * capacity
+    blocks_d, blocks_f = up_ref.shape[0], up_ref.shape[1]
+    tok_count, part = tokens_ref.shape
+    blocks_p = part // BLOCK
+    lanes = up_ref.shape[2]
+    me, t = lax.axis_index("dp"), lax.axis_index("tensor")
+    core, x = t % 2, t // 2
+    sibling, across = 2 * x + 1 - core, 2 * (1 - x) + core
+    others = [(me + k) % groups for k in range(1, groups)]
+
+    load_up = pltpu.make_async_copy(wu_hbm, wu_ref, local_sems.at[0])
+    load_down = pltpu.make_async_copy(wd_hbm, wd_ref, local_sems.at[1])
+    load_up.start()
+    load_down.start()
+
+    barrier = pltpu.get_barrier_semaphore()
+    for j in others:
+        pl.semaphore_signal(barrier, inc=1, device_id={"dp": j}, device_id_type=MESH)
+    for s in (sibling, across):
+        pl.semaphore_signal(barrier, inc=1, device_id={"tensor": s}, device_id_type=MESH)
+
+    pairs = pairs_ref[...]
+    target = lax.rem(pairs, jnp.full_like(pairs, groups))
+    group_of = lax.broadcasted_iota(jnp.int32, (groups, tok_count), 0)
+    match = group_of == target
+    earlier = (
+        lax.broadcasted_iota(jnp.int32, (tok_count, tok_count), 0)
+        < lax.broadcasted_iota(jnp.int32, (tok_count, tok_count), 1)
+    ).astype(jnp.float32).astype(jnp.bfloat16)
+    before = dot(match.astype(jnp.float32).astype(jnp.bfloat16), earlier)
+    spot = before + (group_of * capacity).astype(jnp.float32)
+    position = jnp.sum(jnp.where(match, spot, 0.0), axis=0, keepdims=True)
+    slot_of = lax.broadcasted_iota(jnp.int32, (slots, tok_count), 0).astype(jnp.float32)
+    placed = (slot_of == position).astype(jnp.float32)
+    placer = placed.astype(jnp.bfloat16)
+    placer_turned = placed.T.astype(jnp.bfloat16)
+    known = (lax.broadcasted_iota(jnp.int32, (lanes, tok_count), 0) == pairs).astype(jnp.float32)
+    moved = dot(placer, known.astype(jnp.bfloat16), NT)
+    room = send_p.shape[1] - capacity
+    for j in range(groups):
+        own = moved[j * capacity : (j + 1) * capacity]
+        if room:
+            own = jnp.concatenate([own, jnp.zeros((room, lanes), jnp.float32)], axis=0)
+        send_p[j] = own.astype(jnp.bfloat16)
+    got_p[me] = send_p[me]
+
+    pl.semaphore_wait(barrier, groups + 1)
+
+    def remote(src, dst, sem, where):
+        return pltpu.make_async_remote_copy(
+            src_ref=src, dst_ref=dst, send_sem=ss.at[sem], recv_sem=rs.at[sem],
+            device_id=where, device_id_type=MESH,
+        )
+
+    step = groups - 1
+    every = []
+
+    def launch(copies):
+        for copy in copies:
+            copy.start()
+        every.extend(copies)
+        return copies
+
+    def arrive(copies):
+        for copy in copies:
+            copy.wait_recv()
+
+    trip_p = launch([
+        remote(send_p.at[j], got_p.at[me], k, {"dp": j}) for k, j in enumerate(others)
+    ])
+
+    def dispatch(values_ref, send, got, first):
+        moved = dot(placer, values_ref[...])
+        for j in range(groups):
+            send[j] = stacked(moved, j * capacity, capacity)
+        got[t, me] = send[me]
+        return launch([
+            remote(send.at[j], got.at[t, me], first + k, {"dp": j}) for k, j in enumerate(others)
+        ])
+
+    trip_a = dispatch(tokens_ref, send_a, got_a, step)
+    trip_b = dispatch(cotangent_ref, send_b, got_b, 2 * step)
+    base = 3 * step
+
+    def share(got, first):
+        return launch([
+            remote(got.at[t], got.at[t], first, {"tensor": across}),
+            remote(got.at[t], got.at[t], first + 1, {"tensor": sibling}),
+        ])
+
+    def forward(got, first):
+        return launch([remote(got.at[across], got.at[across], first + 2, {"tensor": sibling})])
+
+    arrive(trip_p)
+    for i in range(groups):
+        unstack(got_p[i, :capacity], wide_ref, i * capacity, 0, capacity)
+    pick = wide_ref[:, :lanes].astype(jnp.bfloat16)
+
+    def expand(table, into_ref, f):
+        bits = dot(pick, table.astype(jnp.float32).astype(jnp.bfloat16), NT).astype(jnp.bfloat16)
+        for d in range(blocks_d):
+            into_ref[f, :, d * BLOCK : (d + 1) * BLOCK] = jnp.broadcast_to(
+                bits[:, d : d + 1], (slots, BLOCK)
+            )
+
+    def expand_up(f, _):
+        expand(up_ref[:, f, :], eu_ref, f)
+        return 0
+
+    def expand_down(f, _):
+        expand(down_ref[f], ed_ref, f)
+        return 0
+
+    lax.fori_loop(0, blocks_f, expand_up, 0)
+    arrive(trip_a)
+    share_a = share(got_a, base)
+    half = blocks_f // 2
+    lax.fori_loop(0, half, expand_down, 0)
+    arrive(share_a[:1])
+    forward_a = forward(got_a, base)
+    lax.fori_loop(half, blocks_f, expand_down, 0)
+    arrive(trip_b)
+    share_b = share(got_b, base + 3)
+    arrive(share_a[1:] + forward_a)
+
+    def assemble(got, into_ref):
+        for s in range(got.shape[0]):
+            for i in range(groups):
+                unstack(got[s, i], wide_ref, i * capacity, s * part, capacity)
+        into_ref[...] = wide_ref[...].astype(jnp.bfloat16)
+
+    assemble(got_a, x_ref)
+    load_up.wait()
+
+    def columns(b):
+        return pl.ds(pl.multiple_of(b * BLOCK, BLOCK), BLOCK)
+
+    def pre_step(f, _):
+        pre = dot(x_ref[...] * eu_ref[f], wu_ref[:, columns(f)])
+        act, slope = gelu_pair(pre)
+        h_ref[:, columns(f)] = act.astype(jnp.bfloat16)
+        slope_ref[:, columns(f)] = slope
+        return 0
+
+    def grad_step(f, _):
+        grad = dot(g_ref[...] * ed_ref[f], wd_ref[columns(f), :], NT)
+        q_ref[:, columns(f)] = (grad * slope_ref[:, columns(f)]).astype(jnp.bfloat16)
+        return 0
+
+    def picked(values_ref, bits_ref, d):
+        return jnp.concatenate(
+            [
+                values_ref[:, f * BLOCK : (f + 1) * BLOCK] * bits_ref[f, :, columns(d)]
+                for f in range(blocks_f)
+            ],
+            axis=1,
+        )
+
+    def mixed_block(d):
+        return dot(picked(h_ref, ed_ref, d), wd_ref[:, columns(d)])
+
+    def input_block(d):
+        return dot(picked(q_ref, eu_ref, d), wu_ref[columns(d), :], NT)
+
+    def total(block, part_ref, sib_ref, out_ref, first):
+        def fill(owner):
+            def one(b, _):
+                part_ref[owner, :, columns(b)] = block(owner * blocks_p + b).astype(jnp.bfloat16)
+                return 0
+
+            lax.fori_loop(0, blocks_p, one, 0)
+
+        sent = []
+        for n, side in enumerate((1 - x, x)):
+            owner = 2 * side + 1 - core
+            fill(owner)
+            sent += launch([
+                remote(part_ref.at[owner], sib_ref.at[side], first + n, {"tensor": sibling})
+            ])
+        fill(across)
+        arrive(sent[:1])
+        out_ref[...] = (
+            part_ref[across].astype(jnp.float32) + sib_ref[1 - x].astype(jnp.float32)
+        ).astype(jnp.bfloat16)
+        return fill, sent[1:]
+
+    def cross(out_ref, in_ref, first):
+        return launch([remote(out_ref, in_ref, first + 2, {"tensor": across})])
+
+    def send_home(part_ref, sib_ref, in_ref, back, home, first):
+        summed = (
+            part_ref[t].astype(jnp.float32)
+            + sib_ref[x].astype(jnp.float32)
+            + in_ref[...].astype(jnp.float32)
+        )
+        for i in range(groups):
+            back[i] = stacked(summed, i * capacity, capacity)
+        home[me] = back[me]
+        return launch([
+            remote(back.at[j], home.at[me], first + k, {"dp": j}) for k, j in enumerate(others)
+        ])
+
+    def finish(home, result_ref):
+        for i in range(groups):
+            unstack(home[i], wide_ref, i * capacity, 0, capacity)
+        result_ref[...] = dot(placer_turned, wide_ref[:, :part].astype(jnp.bfloat16)).astype(jnp.bfloat16)
+
+    lax.fori_loop(0, half, pre_step, 0)
+    arrive(share_b[:1])
+    forward_b = forward(got_b, base + 3)
+    lax.fori_loop(half, blocks_f, pre_step, 0)
+    load_down.wait()
+    fill_m, late_m = total(mixed_block, part_m, sib_m, out_m, base + 6)
+    cross_m = cross(out_m, in_m, base + 6)
+    fill_m(t)
+    arrive(share_b[1:] + forward_b)
+    assemble(got_b, g_ref)
+    lax.fori_loop(0, blocks_f, grad_step, 0)
+    arrive(late_m + cross_m)
+    home_trip_m = send_home(part_m, sib_m, in_m, back_m, home_m, base + 12)
+    fill_i, late_i = total(input_block, part_i, sib_i, out_i, base + 9)
+    cross_i = cross(out_i, in_i, base + 9)
+    fill_i(t)
+    arrive(late_i + cross_i)
+    home_trip_i = send_home(part_i, sib_i, in_i, back_i, home_i, base + 12 + step)
+    arrive(home_trip_m)
+    finish(home_m, mixed_ref)
+    arrive(home_trip_i)
+    finish(home_i, grads_ref)
+    for copy in every:
+        copy.wait_send()
+
+
+def layer(tokens, cotangent, pair_row, up_table, down_table, up_weight, down_weight, groups, capacity, sides):
+    part = tokens.shape[1]
+    slots = groups * capacity
+    width = part * sides
+    hidden = up_weight.shape[1]
+    blocks_f = hidden // BLOCK
+    lanes = up_table.shape[2]
+    tall = capacity * part // BLOCK
+    short = -(-capacity // 16) * 16
+    vmem = pl.BlockSpec(memory_space=pltpu.VMEM)
+    anywhere = pl.BlockSpec(memory_space=pl.ANY)
+    trips = 5 * (groups - 1) + 12
+
+    def buffer(*shape):
+        return pltpu.VMEM(shape, jnp.bfloat16)
+
+    return pl.pallas_call(
+        functools.partial(layer_kernel, groups, capacity),
+        out_shape=[jax.ShapeDtypeStruct(tokens.shape, jnp.bfloat16)] * 2,
+        in_specs=[vmem] * 5 + [anywhere] * 2,
+        out_specs=[vmem] * 2,
+        scratch_shapes=[
+            buffer(*up_weight.shape),
+            buffer(*down_weight.shape),
+            buffer(blocks_f, slots, width),
+            buffer(blocks_f, slots, width),
+            buffer(groups, short, lanes),
+            buffer(groups, tall, BLOCK),
+            buffer(groups, tall, BLOCK),
+            buffer(groups, short, lanes),
+            buffer(sides, groups, tall, BLOCK),
+            buffer(sides, groups, tall, BLOCK),
+            pltpu.VMEM((slots, width), jnp.float32),
+            buffer(slots, width),
+            buffer(slots, width),
+            buffer(slots, hidden),
+            buffer(slots, hidden),
+            pltpu.VMEM((slots, hidden), jnp.float32),
+            buffer(sides, slots, part),
+            buffer(sides, slots, part),
+            buffer(2, slots, part),
+            buffer(2, slots, part),
+            buffer(slots, part),
+            buffer(slots, part),
+            buffer(slots, part),
+            buffer(slots, part),
+            buffer(groups, tall, BLOCK),
+            buffer(groups, tall, BLOCK),
+            buffer(groups, tall, BLOCK),
+            buffer(groups, tall, BLOCK),
+            pltpu.SemaphoreType.DMA((2,)),
+            pltpu.SemaphoreType.DMA((trips,)),
+            pltpu.SemaphoreType.DMA((trips,)),
+        ],
+        compiler_params=pltpu.CompilerParams(
+            collective_id=0, has_side_effects=True, vmem_limit_bytes=60 * 2**20
+        ),
+        name="layer",
+    )(tokens, cotangent, pair_row, up_table, down_table, up_weight, down_weight)
+
+
 def place(pair_ids, groups, capacity):
     target = pair_ids % groups
     matches = (target[:, None] == jnp.arange(groups, dtype=jnp.int32)[None, :]).astype(jnp.int32)
@@ -117,13 +435,19 @@
     pairs = up_mask.shape[0]
     capacity = max(2, (3 * tok_count + 2 * groups - 1) // (2 * groups))
     slot_count = groups * capacity
-    placer = place(pair_ids, groups, capacity)
     lanes = -(-pairs // BLOCK) * BLOCK
-    known = (pair_ids[:, None] == jnp.arange(lanes, dtype=jnp.int32)[None, :]).astype(jnp.bfloat16)
     pad = ((0, 0), (0, 0), (0, lanes - pairs))
     up_table = jnp.pad(jnp.transpose(up_mask, (1, 2, 0)), pad)
     down_table = jnp.pad(jnp.transpose(down_mask, (1, 2, 0)), pad)
-
+    sides = lax.axis_size("tensor")
+    if sides == 4 and capacity * part // BLOCK % 16 == 0 and capacity % 8 == 0:
+        return layer(
+            tokens, cotangent, pair_ids.reshape(1, tok_count), up_table, down_table, up_weight,
+            down_weight[0], groups, capacity, sides,
+        )
+
+    placer = place(pair_ids, groups, capacity)
+    known = (pair_ids[:, None] == jnp.arange(lanes, dtype=jnp.int32)[None, :]).astype(jnp.bfloat16)
     leaving = jnp.concatenate([tokens, cotangent, known], axis=1)
     moved = swap(dot(placer, leaving).astype(jnp.bfloat16), groups, capacity)
     both = jnp.stack([moved[:, :part], moved[:, part : 2 * part]])

time: 146 us -> 73.9 us (0.51)
  waiting for transfers between devices: 46.9 us -> 0 us
  blocking collectives: 37.6 us -> 0 us
  Pallas kernels: 37.5 us -> 66.7 us
  between operations: 14.2 us -> 0.64 us
  other arithmetic: 4.62 us -> 0 us
  local copies, waits for them, and re-layouts: 3.37 us -> 6.28 us
  matrix products: 1.5 us -> 0 us
    all_to_all x2 -> x0, blocking collectives: 37.6 us -> none  [swap(): lax.all_to_all(values.reshape(groups, capacity, width), 'dp', split_axis=...]
    pallas_call x1, Pallas kernels: 37.5 us -> 66.7 us  [layer(): pl.pallas_call(functools.partial(layer_kernel, groups, capacity), out_sha...]
    reduce_scatter x1 -> x0, waiting for transfers between devices: 28.3 us -> none  [per_device(): lax.psum_scatter(jnp.stack([mixed_part, input_part]), 'tensor', scatter_d...]
    all_gather x1 -> x0, waiting for transfers between devices: 18.5 us -> none  [per_device(): whole = lax.all_gather(both, 'tensor', axis=2, tiled=True)]
    unnamed x4 -> x2, local copies, waits for them, and re-layouts: 0.01 us -> 3.14 us
    another operation x3 -> x0, other arithmetic: 2.26 us -> none  [the longest x1 1.3 us: per_device(): jnp.stack([mixed_part, input_part])]
    slice x3 -> x0, local copies, waits for them, and re-layouts: 1.77 us -> none  [the longest x1 1.05 us: per_device(): summed[0]]
    pad x1, local copies, waits for them, and re-layouts: 0.01 us -> 1.57 us  [per_device(): up_table = jnp.pad(jnp.transpose(up_mask, (1, 2, 0)), pad)]
  transfers between devices with their start and end apart: 2 -> 0, of which waited for: 2 -> 0; matrix products, arithmetic and copies ran while one was open for 0% -> 0% of each run, Pallas kernels for 0% -> 0%
where the time goes in v2:
time: 73.9 us; the launch traced here: 73.6 us
  Pallas kernels  66.7 us (90%)
  local copies, waits for them, and re-layouts  6.28 us (8%)
    pallas_call x1, Pallas kernels, layer(): pl.pallas_call(functools.partial(layer_kernel, groups, capacity), out_sha...  66.7 us
    unnamed x2, local copies, waits for them, and re-layouts  3.14 us
    pad x1, local copies, waits for them, and re-layouts, per_device(): up_table = jnp.pad(jnp.transpose(up_mask, (1, 2, 0)), pad)  1.57 us
    pad x1, local copies, waits for them, and re-layouts, per_device(): down_table = jnp.pad(jnp.transpose(down_mask, (1, 2, 0)), pad)  1.57 us

profile of v2, /device:TPU:0, one launch (start us, length us, event | category | flops | bytes accessed | tf_op | source)
XLA Modules:
  0.0 73.6 jit_solution(18169273275825195376)
XLA Ops:
  0.6 1.6 %pad.7.up_ref = s32[16,16,128]{2,1,0:T(8,128)} pad(s32[16,16,100]{2,1,0:T(8,128)} %bitcast.5, s32[]{:T(128)} %constant.0.clone.1), padding=0_0x0_0x0_28 | pad | bytes 233476 | tf_op jit(solution)/shard_map/jit(_pad)/pad | solution.py:440
  2.2 1.6 %pad.8.down_ref = s32[16,16,128]{2,1,0:T(8,128)} pad(s32[16,16,100]{2,1,0:T(8,128)} %bitcast.6, s32[]{:T(128)} %constant.0.clone.1), padding=0_0x0_0x0_28 | pad | bytes 233476 | tf_op jit(solution)/shard_map/jit(_pad)/pad | solution.py:441
  3.8 66.7 %layer.1 = (bf16[128,512]{1,0:T(8,128)(2,1)}, bf16[128,512]{1,0:T(8,128)(2,1)}) custom-call(bf16[128,512]{1,0:T(8,128)(2,1)} %tokens_ref.1, bf16[128,512]{1,0:T(8,128)(2,1)} %cotangent_ref.1, s32[1,128]{1,0:T(1,128)} %bitcast.7, s32[16,16,128]{2,1,0:T(8,128)} %pad.7.up_ref, s32[16,16,128]{2,1,0:T(8,128)} %pad.8.down_ref, bf16[2048,2048]{1,0:T(8,128)(2,1)} %wu_hbm.1, ...), custom_call_target="tpu_custom_call" | custom-call | tf_op jit(solution)/shard_map/layer/pallas_call | solution.py:370
  70.5 1.6 %copy.11 = bf16[128,512]{1,0:T(8,128)(2,1)} copy(bf16[128,512]{1,0:T(8,128)(2,1)} %get-tuple-element.4) | data formatting | bytes 262144
  72.1 1.6 %copy.12 = bf16[128,512]{1,0:T(8,128)(2,1)} copy(bf16[128,512]{1,0:T(8,128)(2,1)} %get-tuple-element.5) | data formatting | bytes 262144

commit v3 on v2

--- a/solution.py
+++ b/solution.py
@@ -112,17 +112,20 @@
         ]
 
 
-def layer_kernel(groups, capacity, tokens_ref, cotangent_ref, pairs_ref, up_ref, down_ref, wu_hbm, wd_hbm,
-                 mixed_ref, grads_ref,
-                 wu_ref, wd_ref, eu_ref, ed_ref, send_p, send_a, send_b, got_p, got_a, got_b,
+def layer_kernel(groups, capacity, tokens_ref, pairs_ref, cotangent_hbm, up_hbm, down_hbm, wu_hbm, wd_hbm,
+                 rows_ref, turned_ref,
+                 wu_ref, wd_ref, up_ref, down_ref, cotangent_ref, eu_ref, ed_ref,
+                 send_p, send_a, send_b, got_p, got_a, got_b,
                  wide_ref, x_ref, g_ref, h_ref, q_ref, slope_ref,
                  part_m, part_i, sib_m, sib_i, out_m, out_i, in_m, in_i,
                  back_m, back_i, home_m, home_i, local_sems, ss, rs):
     slots = groups * capacity
     blocks_d, blocks_f = up_ref.shape[0], up_ref.shape[1]
     tok_count, part = tokens_ref.shape
-    blocks_p = part // BLOCK
-    lanes = up_ref.shape[2]
+    chunks, chunk = part_m.shape[0], part_m.shape[3]
+    blocks_p, blocks_c = part // BLOCK, chunk // BLOCK
+    pair_count = up_ref.shape[2]
+    lanes = send_p.shape[2]
     me, t = lax.axis_index("dp"), lax.axis_index("tensor")
     core, x = t % 2, t // 2
     sibling, across = 2 * x + 1 - core, 2 * (1 - x) + core
@@ -130,6 +133,12 @@
 
     load_up = pltpu.make_async_copy(wu_hbm, wu_ref, local_sems.at[0])
     load_down = pltpu.make_async_copy(wd_hbm, wd_ref, local_sems.at[1])
+    load_ut = pltpu.make_async_copy(up_hbm, up_ref, local_sems.at[2])
+    load_dt = pltpu.make_async_copy(down_hbm, down_ref, local_sems.at[3])
+    load_cot = pltpu.make_async_copy(cotangent_hbm, cotangent_ref, local_sems.at[4])
+    load_ut.start()
+    load_dt.start()
+    load_cot.start()
     load_up.start()
     load_down.start()
 
@@ -153,7 +162,7 @@
     slot_of = lax.broadcasted_iota(jnp.int32, (slots, tok_count), 0).astype(jnp.float32)
     placed = (slot_of == position).astype(jnp.float32)
     placer = placed.astype(jnp.bfloat16)
-    placer_turned = placed.T.astype(jnp.bfloat16)
+    turned_ref[...] = placed.T.astype(jnp.bfloat16)
     known = (lax.broadcasted_iota(jnp.int32, (lanes, tok_count), 0) == pairs).astype(jnp.float32)
     moved = dot(placer, known.astype(jnp.bfloat16), NT)
     room = send_p.shape[1] - capacity
@@ -199,7 +208,6 @@
         ])
 
     trip_a = dispatch(tokens_ref, send_a, got_a, step)
-    trip_b = dispatch(cotangent_ref, send_b, got_b, 2 * step)
     base = 3 * step
 
     def share(got, first):
@@ -214,7 +222,10 @@
     arrive(trip_p)
     for i in range(groups):
         unstack(got_p[i, :capacity], wide_ref, i * capacity, 0, capacity)
-    pick = wide_ref[:, :lanes].astype(jnp.bfloat16)
+    pick = wide_ref[:, :pair_count].astype(jnp.bfloat16)
+    load_ut.wait()
+    load_dt.wait()
+    load_cot.wait()
 
     def expand(table, into_ref, f):
         bits = dot(pick, table.astype(jnp.float32).astype(jnp.bfloat16), NT).astype(jnp.bfloat16)
@@ -223,24 +234,23 @@
                 bits[:, d : d + 1], (slots, BLOCK)
             )
 
-    def expand_up(f, _):
-        expand(up_ref[:, f, :], eu_ref, f)
-        return 0
-
-    def expand_down(f, _):
-        expand(down_ref[f], ed_ref, f)
-        return 0
-
-    lax.fori_loop(0, blocks_f, expand_up, 0)
+    def steps(low, high, at_once, one):
+        def several(n, _):
+            for k in range(at_once):
+                one(low + n * at_once + k)
+            return 0
+
+        lax.fori_loop(0, (high - low) // at_once, several, 0)
+
+    half = blocks_f // 2
+    steps(0, blocks_f, 2, lambda f: expand(up_ref[:, f, :], eu_ref, f))
     arrive(trip_a)
     share_a = share(got_a, base)
-    half = blocks_f // 2
-    lax.fori_loop(0, half, expand_down, 0)
+    trip_b = dispatch(cotangent_ref, send_b, got_b, 2 * step)
+    steps(0, half, 2, lambda f: expand(down_ref[f], ed_ref, f))
     arrive(share_a[:1])
     forward_a = forward(got_a, base)
-    lax.fori_loop(half, blocks_f, expand_down, 0)
-    arrive(trip_b)
-    share_b = share(got_b, base + 3)
+    steps(half, blocks_f, 2, lambda f: expand(down_ref[f], ed_ref, f))
     arrive(share_a[1:] + forward_a)
 
     def assemble(got, into_ref):
@@ -255,17 +265,15 @@
     def columns(b):
         return pl.ds(pl.multiple_of(b * BLOCK, BLOCK), BLOCK)
 
-    def pre_step(f, _):
+    def pre_step(f):
         pre = dot(x_ref[...] * eu_ref[f], wu_ref[:, columns(f)])
         act, slope = gelu_pair(pre)
         h_ref[:, columns(f)] = act.astype(jnp.bfloat16)
         slope_ref[:, columns(f)] = slope
-        return 0
-
-    def grad_step(f, _):
+
+    def grad_step(f):
         grad = dot(g_ref[...] * ed_ref[f], wd_ref[columns(f), :], NT)
         q_ref[:, columns(f)] = (grad * slope_ref[:, columns(f)]).astype(jnp.bfloat16)
-        return 0
 
     def picked(values_ref, bits_ref, d):
         return jnp.concatenate(
@@ -282,73 +290,125 @@
     def input_block(d):
         return dot(picked(q_ref, eu_ref, d), wu_ref[columns(d), :], NT)
 
-    def total(block, part_ref, sib_ref, out_ref, first):
-        def fill(owner):
-            def one(b, _):
-                part_ref[owner, :, columns(b)] = block(owner * blocks_p + b).astype(jnp.bfloat16)
+    class Sums:
+        def __init__(self, block, part_ref, sib_ref, out_ref, in_ref, back_ref, home_ref, first):
+            self.block, self.part, self.sib, self.out = block, part_ref, sib_ref, out_ref
+            self.into, self.back, self.home, self.first = in_ref, back_ref, home_ref, first
+
+        def to_sibling(self, h, n):
+            side = (1 - x, x)[n]
+            return remote(
+                self.part.at[h, 2 * side + 1 - core], self.sib.at[h, side],
+                self.first + h * (3 + step) + n, {"tensor": sibling},
+            )
+
+        def to_across(self, h):
+            return remote(
+                self.out.at[h], self.into.at[h], self.first + h * (3 + step) + 2, {"tensor": across}
+            )
+
+        def to_home(self, h):
+            return [
+                remote(
+                    self.back.at[h, j], self.home.at[h, me],
+                    self.first + h * (3 + step) + 3 + k, {"dp": j},
+                )
+                for k, j in enumerate(others)
+            ]
+
+        def fill(self, h, owner):
+            for b in range(blocks_c):
+                d = owner * blocks_p + h * blocks_c + b
+                self.part[h, owner, :, b * BLOCK : (b + 1) * BLOCK] = self.block(d).astype(jnp.bfloat16)
+
+        def launch_home(self, h):
+            self.to_sibling(h, 1).wait_recv()
+            self.to_across(h).wait_recv()
+            summed = (
+                self.part[h, t].astype(jnp.float32)
+                + self.sib[h, x].astype(jnp.float32)
+                + self.into[h].astype(jnp.float32)
+            )
+            for i in range(groups):
+                self.back[h, i] = stacked(summed, i * capacity, capacity)
+            self.home[h, me] = self.back[h, me]
+            for copy in self.to_home(h):
+                copy.start()
+
+        def run(self, hook):
+            def one(h, _):
+                self.fill(h, 2 * (1 - x) + 1 - core)
+                self.to_sibling(h, 0).start()
+
+                @pl.when(h > 0)
+                def _():
+                    hook()
+                    self.launch_home(h - 1)
+
+                self.fill(h, across)
+                self.to_sibling(h, 0).wait_recv()
+                self.out[h] = (
+                    self.part[h, across].astype(jnp.float32) + self.sib[h, 1 - x].astype(jnp.float32)
+                ).astype(jnp.bfloat16)
+                self.to_across(h).start()
+                self.fill(h, 2 * x + 1 - core)
+                self.to_sibling(h, 1).start()
+                self.fill(h, t)
                 return 0
 
-            lax.fori_loop(0, blocks_p, one, 0)
-
-        sent = []
-        for n, side in enumerate((1 - x, x)):
-            owner = 2 * side + 1 - core
-            fill(owner)
-            sent += launch([
-                remote(part_ref.at[owner], sib_ref.at[side], first + n, {"tensor": sibling})
-            ])
-        fill(across)
-        arrive(sent[:1])
-        out_ref[...] = (
-            part_ref[across].astype(jnp.float32) + sib_ref[1 - x].astype(jnp.float32)
-        ).astype(jnp.bfloat16)
-        return fill, sent[1:]
-
-    def cross(out_ref, in_ref, first):
-        return launch([remote(out_ref, in_ref, first + 2, {"tensor": across})])
-
-    def send_home(part_ref, sib_ref, in_ref, back, home, first):
-        summed = (
-            part_ref[t].astype(jnp.float32)
-            + sib_ref[x].astype(jnp.float32)
-            + in_ref[...].astype(jnp.float32)
-        )
-        for i in range(groups):
-            back[i] = stacked(summed, i * capacity, capacity)
-        home[me] = back[me]
-        return launch([
-            remote(back.at[j], home.at[me], first + k, {"dp": j}) for k, j in enumerate(others)
-        ])
-
-    def finish(home, result_ref):
-        for i in range(groups):
-            unstack(home[i], wide_ref, i * capacity, 0, capacity)
-        result_ref[...] = dot(placer_turned, wide_ref[:, :part].astype(jnp.bfloat16)).astype(jnp.bfloat16)
-
-    lax.fori_loop(0, half, pre_step, 0)
-    arrive(share_b[:1])
-    forward_b = forward(got_b, base + 3)
-    lax.fori_loop(half, blocks_f, pre_step, 0)
+            lax.fori_loop(0, chunks, one, 0)
+
+        def finish(self, n):
+            for h in range(chunks):
+                for copy in self.to_home(h):
+                    copy.wait_recv()
+                for i in range(groups):
+                    unstack(self.home[h, i], wide_ref, i * capacity, h * chunk, capacity)
+            rows_ref[n] = wide_ref[:, :part].astype(jnp.bfloat16)
+
+        def settle(self):
+            for h in range(chunks):
+                for copy in [self.to_sibling(h, 0), self.to_sibling(h, 1), self.to_across(h)] + self.to_home(h):
+                    copy.wait_send()
+
+    sums_m = Sums(mixed_block, part_m, sib_m, out_m, in_m, back_m, home_m, base + 6)
+    sums_i = Sums(
+        input_block, part_i, sib_i, out_i, in_i, back_i, home_i, base + 6 + chunks * (3 + step)
+    )
+
+    steps(0, half, 4, pre_step)
+    arrive(trip_b)
+    share_b = share(got_b, base + 3)
+    steps(half, blocks_f, 4, pre_step)
     load_down.wait()
-    fill_m, late_m = total(mixed_block, part_m, sib_m, out_m, base + 6)
-    cross_m = cross(out_m, in_m, base + 6)
-    fill_m(t)
-    arrive(share_b[1:] + forward_b)
+    forward_b = remote(got_b.at[across], got_b.at[across], base + 5, {"tensor": sibling})
+
+    def pass_on():
+        share_b[0].wait_recv()
+        forward_b.start()
+
+    sums_m.run(pass_on)
+    share_b[1].wait_recv()
+    forward_b.wait_recv()
     assemble(got_b, g_ref)
-    lax.fori_loop(0, blocks_f, grad_step, 0)
-    arrive(late_m + cross_m)
-    home_trip_m = send_home(part_m, sib_m, in_m, back_m, home_m, base + 12)
-    fill_i, late_i = total(input_block, part_i, sib_i, out_i, base + 9)
-    cross_i = cross(out_i, in_i, base + 9)
-    fill_i(t)
-    arrive(late_i + cross_i)
-    home_trip_i = send_home(part_i, sib_i, in_i, back_i, home_i, base + 12 + step)
-    arrive(home_trip_m)
-    finish(home_m, mixed_ref)
-    arrive(home_trip_i)
-    finish(home_i, grads_ref)
+    steps(0, half, 4, grad_step)
+    sums_m.launch_home(chunks - 1)
+    steps(half, blocks_f, 4, grad_step)
+    sums_i.run(lambda: None)
+    sums_i.launch_home(chunks - 1)
+    sums_m.finish(0)
+    sums_i.finish(1)
     for copy in every:
         copy.wait_send()
+    forward_b.wait_send()
+    sums_m.settle()
+    sums_i.settle()
+
+
+def settle_kernel(rows_ref, turned_ref, mixed_ref, grads_ref):
+    turned = turned_ref[...]
+    mixed_ref[...] = dot(turned, rows_ref[0]).astype(jnp.bfloat16)
+    grads_ref[...] = dot(turned, rows_ref[1]).astype(jnp.bfloat16)
 
 
 def layer(tokens, cotangent, pair_row, up_table, down_table, up_weight, down_weight, groups, capacity, sides):
@@ -357,24 +417,32 @@
     width = part * sides
     hidden = up_weight.shape[1]
     blocks_f = hidden // BLOCK
-    lanes = up_table.shape[2]
+    lanes = -(-up_table.shape[2] // BLOCK) * BLOCK
+    chunks = 2
+    chunk = part // chunks
     tall = capacity * part // BLOCK
     short = -(-capacity // 16) * 16
     vmem = pl.BlockSpec(memory_space=pltpu.VMEM)
     anywhere = pl.BlockSpec(memory_space=pl.ANY)
-    trips = 5 * (groups - 1) + 12
+    trips = 3 * (groups - 1) + 6 + 2 * chunks * (groups + 2)
 
     def buffer(*shape):
         return pltpu.VMEM(shape, jnp.bfloat16)
 
-    return pl.pallas_call(
+    rows, turned = pl.pallas_call(
         functools.partial(layer_kernel, groups, capacity),
-        out_shape=[jax.ShapeDtypeStruct(tokens.shape, jnp.bfloat16)] * 2,
-        in_specs=[vmem] * 5 + [anywhere] * 2,
+        out_shape=[
+            jax.ShapeDtypeStruct((2, slots, part), jnp.bfloat16),
+            jax.ShapeDtypeStruct((tokens.shape[0], slots), jnp.bfloat16),
+        ],
+        in_specs=[vmem] * 2 + [anywhere] * 5,
         out_specs=[vmem] * 2,
         scratch_shapes=[
             buffer(*up_weight.shape),
             buffer(*down_weight.shape),
+            pltpu.VMEM(up_table.shape, jnp.int32),
+            pltpu.VMEM(down_table.shape, jnp.int32),
+            buffer(*cotangent.shape),
             buffer(blocks_f, slots, width),
             buffer(blocks_f, slots, width),
             buffer(groups, short, lanes),
@@ -389,19 +457,19 @@
             buffer(slots, hidden),
             buffer(slots, hidden),
             pltpu.VMEM((slots, hidden), jnp.float32),
-            buffer(sides, slots, part),
-            buffer(sides, slots, part),
-            buffer(2, slots, part),
-            buffer(2, slots, part),
-            buffer(slots, part),
-            buffer(slots, part),
-            buffer(slots, part),
-            buffer(slots, part),
-            buffer(groups, tall, BLOCK),
-            buffer(groups, tall, BLOCK),
-            buffer(groups, tall, BLOCK),
-            buffer(groups, tall, BLOCK),
-            pltpu.SemaphoreType.DMA((2,)),
+            buffer(chunks, sides, slots, chunk),
+            buffer(chunks, sides, slots, chunk),
+            buffer(chunks, 2, slots, chunk),
+            buffer(chunks, 2, slots, chunk),
+            buffer(chunks, slots, chunk),
+            buffer(chunks, slots, chunk),
+            buffer(chunks, slots, chunk),
+            buffer(chunks, slots, chunk),
+            buffer(chunks, groups, tall // chunks, BLOCK),
+            buffer(chunks, groups, tall // chunks, BLOCK),
+            buffer(chunks, groups, tall // chunks, BLOCK),
+            buffer(chunks, groups, tall // chunks, BLOCK),
+            pltpu.SemaphoreType.DMA((5,)),
             pltpu.SemaphoreType.DMA((trips,)),
             pltpu.SemaphoreType.DMA((trips,)),
         ],
@@ -409,7 +477,14 @@
             collective_id=0, has_side_effects=True, vmem_limit_bytes=60 * 2**20
         ),
         name="layer",
-    )(tokens, cotangent, pair_row, up_table, down_table, up_weight, down_weight)
+    )(tokens, pair_row, cotangent, up_table, down_table, up_weight, down_weight)
+    return pl.pallas_call(
+        settle_kernel,
+        out_shape=[jax.ShapeDtypeStruct(tokens.shape, jnp.bfloat16)] * 2,
+        in_specs=[vmem] * 2,
+        out_specs=[vmem] * 2,
+        name="settle",
+    )(rows, turned)
 
 
 def place(pair_ids, groups, capacity):
@@ -437,10 +512,10 @@
     slot_count = groups * capacity
     lanes = -(-pairs // BLOCK) * BLOCK
     pad = ((0, 0), (0, 0), (0, lanes - pairs))
-    up_table = jnp.pad(jnp.transpose(up_mask, (1, 2, 0)), pad)
-    down_table = jnp.pad(jnp.transpose(down_mask, (1, 2, 0)), pad)
+    up_table = jnp.transpose(up_mask, (1, 2, 0))
+    down_table = jnp.transpose(down_mask, (1, 2, 0))
     sides = lax.axis_size("tensor")
-    if sides == 4 and capacity * part // BLOCK % 16 == 0 and capacity % 8 == 0:
+    if sides == 4 and part % 256 == 0 and capacity * part // 256 % 16 == 0 and capacity % 8 == 0:
         return layer(
             tokens, cotangent, pair_ids.reshape(1, tok_count), up_table, down_table, up_weight,
             down_weight[0], groups, capacity, sides,
@@ -453,7 +528,7 @@
     both = jnp.stack([moved[:, :part], moved[:, part : 2 * part]])
     whole = lax.all_gather(both, "tensor", axis=2, tiled=True)
     mixed_part, input_part = compute(
-        whole[0], whole[1], moved[:, 2 * part :], up_table, down_table, up_weight, down_weight[0]
+        whole[0], whole[1], moved[:, 2 * part :], jnp.pad(up_table, pad), jnp.pad(down_table, pad), up_weight, down_weight[0]
     )
     summed = lax.psum_scatter(
         jnp.stack([mixed_part, input_part]), "tensor", scatter_dimension=2, tiled=True

time: 73.9 us -> 64.2 us (0.87)
  local copies, waits for them, and re-layouts: 6.28 us -> 0 us
  Pallas kernels: 66.7 us -> 63.4 us
    pallas_call x1, Pallas kernels: 66.7 us -> 61.5 us  [layer(): pl.pallas_call(functools.partial(layer_kernel, groups, capacity), out_sha...]
    pad x2 -> x0, local copies, waits for them, and re-layouts: 3.14 us -> none  [the longest x1 1.57 us: per_device(): up_table = jnp.pad(jnp.transpose(up_mask, (1, 2, 0)), pad)]
    unnamed x2 -> x0, local copies, waits for them, and re-layouts: 3.14 us -> none
    pallas_call x0 -> x1, Pallas kernels: none -> 1.88 us  [layer(): pl.pallas_call(settle_kernel, out_shape=[jax.ShapeDtypeStruct(tokens.shap...]
where the time goes in v3:
time: 64.2 us; the launch traced here: 64 us
  Pallas kernels  63.4 us (99%)
    pallas_call x1, Pallas kernels, layer(): pl.pallas_call(functools.partial(layer_kernel, groups, capacity), out_sha...  61.5 us
    pallas_call x1, Pallas kernels, layer(): pl.pallas_call(settle_kernel, out_shape=[jax.ShapeDtypeStruct(tokens.shap...  1.88 us

profile of v3, /device:TPU:0, one launch (start us, length us, event | category | flops | bytes accessed | tf_op | source)
XLA Modules:
  0.0 64.0 jit_solution(5700180084834706896)
XLA Ops:
  0.6 61.5 %layer.1 = (bf16[2,192,512]{2,1,0:T(8,128)(2,1)}, bf16[128,192]{1,0:T(8,128)(2,1)}) custom-call(bf16[128,512]{1,0:T(8,128)(2,1)} %tokens_ref.1, s32[1,128]{1,0:T(1,128)} %bitcast.7, bf16[128,512]{1,0:T(8,128)(2,1)} %cotangent_hbm.1, s32[16,16,100]{2,1,0:T(8,128)} %bitcast.5, s32[16,16,100]{2,1,0:T(8,128)} %bitcast.6, bf16[2048,2048]{1,0:T(8,128)(2,1)} %wu_hbm.1, ...), custom_call_target="tpu_custom_call" | custom-call | tf_op jit(solution)/shard_map/layer/pallas_call | solution.py:432
  62.2 1.9 %settle.1 = (bf16[128,512]{1,0:T(8,128)(2,1)}, bf16[128,512]{1,0:T(8,128)(2,1)}) custom-call(bf16[2,192,512]{2,1,0:T(8,128)(2,1)} %get-tuple-element.4.rows_ref, bf16[128,192]{1,0:T(8,128)(2,1)} %get-tuple-element.5.turned_ref), custom_call_target="tpu_custom_call" | custom-call | tf_op jit(solution)/shard_map/settle/pallas_call | solution.py:481

commit v4 on v3

--- a/solution.py
+++ b/solution.py
@@ -8,6 +8,7 @@
 from jax.sharding import PartitionSpec as P
 
 BLOCK = 128
+TILE = 256
 ROOT = 0.7978845608028654
 CUBE = 0.044715
 NT = (((1,), (1,)), ((), ()))
@@ -265,30 +266,55 @@
     def columns(b):
         return pl.ds(pl.multiple_of(b * BLOCK, BLOCK), BLOCK)
 
+    def tiled(depth, left, right, dims):
+        sums = None
+        for k in range(0, depth, TILE):
+            one = dot(left(k), right(k), dims)
+            sums = one if sums is None else sums + one
+        return sums
+
+    def cut(k):
+        return slice(k, k + TILE)
+
     def pre_step(f):
-        pre = dot(x_ref[...] * eu_ref[f], wu_ref[:, columns(f)])
+        pre = tiled(
+            x_ref.shape[1],
+            lambda k: x_ref[:, cut(k)] * eu_ref[f, :, cut(k)],
+            lambda k: wu_ref[cut(k), columns(f)],
+            NN,
+        )
         act, slope = gelu_pair(pre)
         h_ref[:, columns(f)] = act.astype(jnp.bfloat16)
         slope_ref[:, columns(f)] = slope
 
     def grad_step(f):
-        grad = dot(g_ref[...] * ed_ref[f], wd_ref[columns(f), :], NT)
+        grad = tiled(
+            g_ref.shape[1],
+            lambda k: g_ref[:, cut(k)] * ed_ref[f, :, cut(k)],
+            lambda k: wd_ref[columns(f), cut(k)],
+            NT,
+        )
         q_ref[:, columns(f)] = (grad * slope_ref[:, columns(f)]).astype(jnp.bfloat16)
 
-    def picked(values_ref, bits_ref, d):
-        return jnp.concatenate(
-            [
-                values_ref[:, f * BLOCK : (f + 1) * BLOCK] * bits_ref[f, :, columns(d)]
-                for f in range(blocks_f)
-            ],
-            axis=1,
+    def picked(values_ref, bits_ref, d, k):
+        bits = [bits_ref[f, :, columns(d)] for f in range(k // BLOCK, (k + TILE) // BLOCK)]
+        return values_ref[:, cut(k)] * jnp.concatenate(bits, axis=1)
+
+    def mixed_block(d):
+        return tiled(
+            h_ref.shape[1],
+            lambda k: picked(h_ref, ed_ref, d, k),
+            lambda k: wd_ref[cut(k), columns(d)],
+            NN,
         )
 
-    def mixed_block(d):
-        return dot(picked(h_ref, ed_ref, d), wd_ref[:, columns(d)])
-
     def input_block(d):
-        return dot(picked(q_ref, eu_ref, d), wu_ref[columns(d), :], NT)
+        return tiled(
+            q_ref.shape[1],
+            lambda k: picked(q_ref, eu_ref, d, k),
+            lambda k: wu_ref[columns(d), cut(k)],
+            NT,
+        )
 
     class Sums:
         def __init__(self, block, part_ref, sib_ref, out_ref, in_ref, back_ref, home_ref, first):

time: 64.2 us -> 64.3 us (level)
  no operation moved by 1% of the time
where the time goes in v4:
time: 64.3 us; the launch traced here: 64.1 us
  Pallas kernels  63.5 us (99%)
    pallas_call x1, Pallas kernels, layer(): pl.pallas_call(functools.partial(layer_kernel, groups, capacity), out_sha...  61.6 us
    pallas_call x1, Pallas kernels, layer(): pl.pallas_call(settle_kernel, out_shape=[jax.ShapeDtypeStruct(tokens.shap...  1.88 us

profile of v4, /device:TPU:0, one launch (start us, length us, event | category | flops | bytes accessed | tf_op | source)
XLA Modules:
  0.0 64.1 jit_solution(8291621452460356099)
XLA Ops:
  0.6 61.6 %layer.1 = (bf16[2,192,512]{2,1,0:T(8,128)(2,1)}, bf16[128,192]{1,0:T(8,128)(2,1)}) custom-call(bf16[128,512]{1,0:T(8,128)(2,1)} %tokens_ref.1, s32[1,128]{1,0:T(1,128)} %bitcast.7, bf16[128,512]{1,0:T(8,128)(2,1)} %cotangent_hbm.1, s32[16,16,100]{2,1,0:T(8,128)} %bitcast.5, s32[16,16,100]{2,1,0:T(8,128)} %bitcast.6, bf16[2048,2048]{1,0:T(8,128)(2,1)} %wu_hbm.1, ...), custom_call_target="tpu_custom_call" | custom-call | tf_op jit(solution)/shard_map/layer/pallas_call | solution.py:458
  62.2 1.9 %settle.1 = (bf16[128,512]{1,0:T(8,128)(2,1)}, bf16[128,512]{1,0:T(8,128)(2,1)}) custom-call(bf16[2,192,512]{2,1,0:T(8,128)(2,1)} %get-tuple-element.4.rows_ref, bf16[128,192]{1,0:T(8,128)(2,1)} %get-tuple-element.5.turned_ref), custom_call_target="tpu_custom_call" | custom-call | tf_op jit(solution)/shard_map/settle/pallas_call | solution.py:507

commit v5 on v3

--- a/solution.py
+++ b/solution.py
@@ -234,9 +234,9 @@
                 bits[:, d : d + 1], (slots, BLOCK)
             )
 
-    def steps(low, high, at_once, one):
+    def steps(low, high, at_once, one, stride=1):
         def several(n, _):
-            for k in range(at_once):
+            for k in range(0, at_once, stride):
                 one(low + n * at_once + k)
             return 0
 
@@ -265,15 +265,25 @@
     def columns(b):
         return pl.ds(pl.multiple_of(b * BLOCK, BLOCK), BLOCK)
 
+    def double(b):
+        return pl.ds(pl.multiple_of(b * BLOCK, 2 * BLOCK), 2 * BLOCK)
+
+    def quarters(rows_of, weights, dims):
+        tall = jnp.concatenate([rows_of(0), rows_of(1)], axis=0)
+        square = dot(tall, weights, dims)
+        return square[:slots, :BLOCK], square[slots:, BLOCK:]
+
     def pre_step(f):
-        pre = dot(x_ref[...] * eu_ref[f], wu_ref[:, columns(f)])
-        act, slope = gelu_pair(pre)
-        h_ref[:, columns(f)] = act.astype(jnp.bfloat16)
-        slope_ref[:, columns(f)] = slope
+        both = quarters(lambda n: x_ref[...] * eu_ref[f + n], wu_ref[:, double(f)], NN)
+        for n, pre in enumerate(both):
+            act, slope = gelu_pair(pre)
+            h_ref[:, columns(f + n)] = act.astype(jnp.bfloat16)
+            slope_ref[:, columns(f + n)] = slope
 
     def grad_step(f):
-        grad = dot(g_ref[...] * ed_ref[f], wd_ref[columns(f), :], NT)
-        q_ref[:, columns(f)] = (grad * slope_ref[:, columns(f)]).astype(jnp.bfloat16)
+        both = quarters(lambda n: g_ref[...] * ed_ref[f + n], wd_ref[double(f), :], NT)
+        for n, grad in enumerate(both):
+            q_ref[:, columns(f + n)] = (grad * slope_ref[:, columns(f + n)]).astype(jnp.bfloat16)
 
     def picked(values_ref, bits_ref, d):
         return jnp.concatenate(
@@ -284,11 +294,11 @@
             axis=1,
         )
 
-    def mixed_block(d):
-        return dot(picked(h_ref, ed_ref, d), wd_ref[:, columns(d)])
-
-    def input_block(d):
-        return dot(picked(q_ref, eu_ref, d), wu_ref[columns(d), :], NT)
+    def mixed_pair(d):
+        return quarters(lambda n: picked(h_ref, ed_ref, d + n), wd_ref[:, double(d)], NN)
+
+    def input_pair(d):
+        return quarters(lambda n: picked(q_ref, eu_ref, d + n), wu_ref[double(d), :], NT)
 
     class Sums:
         def __init__(self, block, part_ref, sib_ref, out_ref, in_ref, back_ref, home_ref, first):
@@ -317,9 +327,11 @@
             ]
 
         def fill(self, h, owner):
-            for b in range(blocks_c):
-                d = owner * blocks_p + h * blocks_c + b
-                self.part[h, owner, :, b * BLOCK : (b + 1) * BLOCK] = self.block(d).astype(jnp.bfloat16)
+            for b in range(0, blocks_c, 2):
+                both = self.block(owner * blocks_p + h * blocks_c + b)
+                for n, value in enumerate(both):
+                    at = (b + n) * BLOCK
+                    self.part[h, owner, :, at : at + BLOCK] = value.astype(jnp.bfloat16)
 
         def launch_home(self, h):
             self.to_sibling(h, 1).wait_recv()
@@ -371,15 +383,15 @@
                 for copy in [self.to_sibling(h, 0), self.to_sibling(h, 1), self.to_across(h)] + self.to_home(h):
                     copy.wait_send()
 
-    sums_m = Sums(mixed_block, part_m, sib_m, out_m, in_m, back_m, home_m, base + 6)
+    sums_m = Sums(mixed_pair, part_m, sib_m, out_m, in_m, back_m, home_m, base + 6)
     sums_i = Sums(
-        input_block, part_i, sib_i, out_i, in_i, back_i, home_i, base + 6 + chunks * (3 + step)
+        input_pair, part_i, sib_i, out_i, in_i, back_i, home_i, base + 6 + chunks * (3 + step)
     )
 
-    steps(0, half, 4, pre_step)
+    steps(0, half, 4, pre_step, 2)
     arrive(trip_b)
     share_b = share(got_b, base + 3)
-    steps(half, blocks_f, 4, pre_step)
+    steps(half, blocks_f, 4, pre_step, 2)
     load_down.wait()
     forward_b = remote(got_b.at[across], got_b.at[across], base + 5, {"tensor": sibling})
 
@@ -391,9 +403,9 @@
     share_b[1].wait_recv()
     forward_b.wait_recv()
     assemble(got_b, g_ref)
-    steps(0, half, 4, grad_step)
+    steps(0, half, 4, grad_step, 2)
     sums_m.launch_home(chunks - 1)
-    steps(half, blocks_f, 4, grad_step)
+    steps(half, blocks_f, 4, grad_step, 2)
     sums_i.run(lambda: None)
     sums_i.launch_home(chunks - 1)
     sums_m.finish(0)
@@ -515,7 +527,7 @@
     up_table = jnp.transpose(up_mask, (1, 2, 0))
     down_table = jnp.transpose(down_mask, (1, 2, 0))
     sides = lax.axis_size("tensor")
-    if sides == 4 and part % 256 == 0 and capacity * part // 256 % 16 == 0 and capacity % 8 == 0:
+    if sides == 4 and part % 512 == 0 and up_weight.shape[1] % 1024 == 0 and capacity * part // 256 % 16 == 0 and capacity % 8 == 0:
         return layer(
             tokens, cotangent, pair_ids.reshape(1, tok_count), up_table, down_table, up_weight,
             down_weight[0], groups, capacity, sides,

time: 64.2 us -> 64 us (level)
  no operation moved by 1% of the time
where the time goes in v5:
time: 64 us; the launch traced here: 63.9 us
  Pallas kernels  63.2 us (99%)
  between operations  0.64 us (1%)
    pallas_call x1, Pallas kernels, layer(): pl.pallas_call(functools.partial(layer_kernel, groups, capacity), out_sha...  61.4 us
    pallas_call x1, Pallas kernels, layer(): pl.pallas_call(settle_kernel, out_shape=[jax.ShapeDtypeStruct(tokens.shap...  1.88 us

profile of v5, /device:TPU:0, one launch (start us, length us, event | category | flops | bytes accessed | tf_op | source)
XLA Modules:
  0.0 63.9 jit_solution(9496413326579614858)
XLA Ops:
  0.6 61.4 %layer.1 = (bf16[2,192,512]{2,1,0:T(8,128)(2,1)}, bf16[128,192]{1,0:T(8,128)(2,1)}) custom-call(bf16[128,512]{1,0:T(8,128)(2,1)} %tokens_ref.1, s32[1,128]{1,0:T(1,128)} %bitcast.7, bf16[128,512]{1,0:T(8,128)(2,1)} %cotangent_hbm.1, s32[16,16,100]{2,1,0:T(8,128)} %bitcast.5, s32[16,16,100]{2,1,0:T(8,128)} %bitcast.6, bf16[2048,2048]{1,0:T(8,128)(2,1)} %wu_hbm.1, ...), custom_call_target="tpu_custom_call" | custom-call | tf_op jit(solution)/shard_map/layer/pallas_call | solution.py:444
  62.0 1.9 %settle.1 = (bf16[128,512]{1,0:T(8,128)(2,1)}, bf16[128,512]{1,0:T(8,128)(2,1)}) custom-call(bf16[2,192,512]{2,1,0:T(8,128)(2,1)} %get-tuple-element.4.rows_ref, bf16[128,192]{1,0:T(8,128)(2,1)} %get-tuple-element.5.turned_ref), custom_call_target="tpu_custom_call" | custom-call | tf_op jit(solution)/shard_map/settle/pallas_call | solution.py:493

commit v6 on v3

--- a/solution.py
+++ b/solution.py
@@ -122,8 +122,7 @@
     slots = groups * capacity
     blocks_d, blocks_f = up_ref.shape[0], up_ref.shape[1]
     tok_count, part = tokens_ref.shape
-    chunks, chunk = part_m.shape[0], part_m.shape[3]
-    blocks_p, blocks_c = part // BLOCK, chunk // BLOCK
+    blocks_p = part // BLOCK
     pair_count = up_ref.shape[2]
     lanes = send_p.shape[2]
     me, t = lax.axis_index("dp"), lax.axis_index("tensor")
@@ -173,6 +172,13 @@
         send_p[j] = own.astype(jnp.bfloat16)
     got_p[me] = send_p[me]
 
+    def pack(values_ref, send, got):
+        moved = dot(placer, values_ref[...])
+        for j in range(groups):
+            send[j] = stacked(moved, j * capacity, capacity)
+        got[t, me] = send[me]
+
+    pack(tokens_ref, send_a, got_a)
     pl.semaphore_wait(barrier, groups + 1)
 
     def remote(src, dst, sem, where):
@@ -198,16 +204,12 @@
         remote(send_p.at[j], got_p.at[me], k, {"dp": j}) for k, j in enumerate(others)
     ])
 
-    def dispatch(values_ref, send, got, first):
-        moved = dot(placer, values_ref[...])
-        for j in range(groups):
-            send[j] = stacked(moved, j * capacity, capacity)
-        got[t, me] = send[me]
+    def dispatch(send, got, first):
         return launch([
             remote(send.at[j], got.at[t, me], first + k, {"dp": j}) for k, j in enumerate(others)
         ])
 
-    trip_a = dispatch(tokens_ref, send_a, got_a, step)
+    trip_a = dispatch(send_a, got_a, step)
     base = 3 * step
 
     def share(got, first):
@@ -234,9 +236,9 @@
                 bits[:, d : d + 1], (slots, BLOCK)
             )
 
-    def steps(low, high, at_once, one):
+    def steps(low, high, at_once, one, stride=1):
         def several(n, _):
-            for k in range(at_once):
+            for k in range(0, at_once, stride):
                 one(low + n * at_once + k)
             return 0
 
@@ -244,13 +246,13 @@
 
     half = blocks_f // 2
     steps(0, blocks_f, 2, lambda f: expand(up_ref[:, f, :], eu_ref, f))
+    pack(cotangent_ref, send_b, got_b)
     arrive(trip_a)
     share_a = share(got_a, base)
-    trip_b = dispatch(cotangent_ref, send_b, got_b, 2 * step)
+    trip_b = dispatch(send_b, got_b, 2 * step)
     steps(0, half, 2, lambda f: expand(down_ref[f], ed_ref, f))
     arrive(share_a[:1])
     forward_a = forward(got_a, base)
-    steps(half, blocks_f, 2, lambda f: expand(down_ref[f], ed_ref, f))
     arrive(share_a[1:] + forward_a)
 
     def assemble(got, into_ref):
@@ -270,6 +272,11 @@
         act, slope = gelu_pair(pre)
         h_ref[:, columns(f)] = act.astype(jnp.bfloat16)
         slope_ref[:, columns(f)] = slope
+
+    def pre_pair(f):
+        expand(down_ref[half + f // 2], ed_ref, half + f // 2)
+        pre_step(f)
+        pre_step(f + 1)
 
     def grad_step(f):
         grad = dot(g_ref[...] * ed_ref[f], wd_ref[columns(f), :], NT)
@@ -294,6 +301,8 @@
         def __init__(self, block, part_ref, sib_ref, out_ref, in_ref, back_ref, home_ref, first):
             self.block, self.part, self.sib, self.out = block, part_ref, sib_ref, out_ref
             self.into, self.back, self.home, self.first = in_ref, back_ref, home_ref, first
+            self.chunks, self.chunk = part_ref.shape[0], part_ref.shape[3]
+            self.blocks = self.chunk // BLOCK
 
         def to_sibling(self, h, n):
             side = (1 - x, x)[n]
@@ -317,8 +326,8 @@
             ]
 
         def fill(self, h, owner):
-            for b in range(blocks_c):
-                d = owner * blocks_p + h * blocks_c + b
+            for b in range(self.blocks):
+                d = owner * blocks_p + h * self.blocks + b
                 self.part[h, owner, :, b * BLOCK : (b + 1) * BLOCK] = self.block(d).astype(jnp.bfloat16)
 
         def launch_home(self, h):
@@ -340,10 +349,8 @@
                 self.fill(h, 2 * (1 - x) + 1 - core)
                 self.to_sibling(h, 0).start()
 
-                @pl.when(h > 0)
-                def _():
-                    hook()
-                    self.launch_home(h - 1)
+                if self.chunks > 1:
+                    pl.when(h > 0)(lambda: self.launch_home(h - 1))
 
                 self.fill(h, across)
                 self.to_sibling(h, 0).wait_recv()
@@ -351,35 +358,36 @@
                     self.part[h, across].astype(jnp.float32) + self.sib[h, 1 - x].astype(jnp.float32)
                 ).astype(jnp.bfloat16)
                 self.to_across(h).start()
+                hook()
                 self.fill(h, 2 * x + 1 - core)
                 self.to_sibling(h, 1).start()
                 self.fill(h, t)
                 return 0
 
-            lax.fori_loop(0, chunks, one, 0)
+            lax.fori_loop(0, self.chunks, one, 0)
 
         def finish(self, n):
-            for h in range(chunks):
+            for h in range(self.chunks):
                 for copy in self.to_home(h):
                     copy.wait_recv()
                 for i in range(groups):
-                    unstack(self.home[h, i], wide_ref, i * capacity, h * chunk, capacity)
+                    unstack(self.home[h, i], wide_ref, i * capacity, h * self.chunk, capacity)
             rows_ref[n] = wide_ref[:, :part].astype(jnp.bfloat16)
 
         def settle(self):
-            for h in range(chunks):
+            for h in range(self.chunks):
                 for copy in [self.to_sibling(h, 0), self.to_sibling(h, 1), self.to_across(h)] + self.to_home(h):
                     copy.wait_send()
 
     sums_m = Sums(mixed_block, part_m, sib_m, out_m, in_m, back_m, home_m, base + 6)
     sums_i = Sums(
-        input_block, part_i, sib_i, out_i, in_i, back_i, home_i, base + 6 + chunks * (3 + step)
+        input_block, part_i, sib_i, out_i, in_i, back_i, home_i, base + 6 + part_m.shape[0] * (3 + step)
     )
 
-    steps(0, half, 4, pre_step)
+    steps(0, half, 4, pre_pair, 2)
     arrive(trip_b)
     share_b = share(got_b, base + 3)
-    steps(half, blocks_f, 4, pre_step)
+    steps(half, blocks_f, 4, pre_pair, 2)
     load_down.wait()
     forward_b = remote(got_b.at[across], got_b.at[across], base + 5, {"tensor": sibling})
 
@@ -392,16 +400,16 @@
     forward_b.wait_recv()
     assemble(got_b, g_ref)
     steps(0, half, 4, grad_step)
-    sums_m.launch_home(chunks - 1)
+    sums_m.launch_home(sums_m.chunks - 1)
     steps(half, blocks_f, 4, grad_step)
     sums_i.run(lambda: None)
-    sums_i.launch_home(chunks - 1)
+    sums_i.launch_home(sums_i.chunks - 1)
     sums_m.finish(0)
-    sums_i.finish(1)
     for copy in every:
         copy.wait_send()
     forward_b.wait_send()
     sums_m.settle()
+    sums_i.finish(1)
     sums_i.settle()
 
 
@@ -418,13 +426,12 @@
     hidden = up_weight.shape[1]
     blocks_f = hidden // BLOCK
     lanes = -(-up_table.shape[2] // BLOCK) * BLOCK
-    chunks = 2
-    chunk = part // chunks
+    chunks = (1, 2)
     tall = capacity * part // BLOCK
     short = -(-capacity // 16) * 16
     vmem = pl.BlockSpec(memory_space=pltpu.VMEM)
     anywhere = pl.BlockSpec(memory_space=pl.ANY)
-    trips = 3 * (groups - 1) + 6 + 2 * chunks * (groups + 2)
+    trips = 3 * (groups - 1) + 6 + sum(chunks) * (groups + 2)
 
     def buffer(*shape):
         return pltpu.VMEM(shape, jnp.bfloat16)
@@ -457,18 +464,10 @@
             buffer(slots, hidden),
             buffer(slots, hidden),
             pltpu.VMEM((slots, hidden), jnp.float32),
-            buffer(chunks, sides, slots, chunk),
-            buffer(chunks, sides, slots, chunk),
-            buffer(chunks, 2, slots, chunk),
-            buffer(chunks, 2, slots, chunk),
-            buffer(chunks, slots, chunk),
-            buffer(chunks, slots, chunk),
-            buffer(chunks, slots, chunk),
-            buffer(chunks, slots, chunk),
-            buffer(chunks, groups, tall // chunks, BLOCK),
-            buffer(chunks, groups, tall // chunks, BLOCK),
-            buffer(chunks, groups, tall // chunks, BLOCK),
-            buffer(chunks, groups, tall // chunks, BLOCK),
+            *[buffer(n, sides, slots, part // n) for n in chunks],
+            *[buffer(n, 2, slots, part // n) for n in chunks],
+            *[buffer(n, slots, part // n) for n in chunks * 2],
+            *[buffer(n, groups, tall // n, BLOCK) for n in chunks * 2],
             pltpu.SemaphoreType.DMA((5,)),
             pltpu.SemaphoreType.DMA((trips,)),
             pltpu.SemaphoreType.DMA((trips,)),
@@ -515,7 +514,7 @@
     up_table = jnp.transpose(up_mask, (1, 2, 0))
     down_table = jnp.transpose(down_mask, (1, 2, 0))
     sides = lax.axis_size("tensor")
-    if sides == 4 and part % 256 == 0 and capacity * part // 256 % 16 == 0 and capacity % 8 == 0:
+    if sides == 4 and part % 256 == 0 and up_weight.shape[1] % 1024 == 0 and capacity * part // 256 % 16 == 0 and capacity % 8 == 0:
         return layer(
             tokens, cotangent, pair_ids.reshape(1, tok_count), up_table, down_table, up_weight,
             down_weight[0], groups, capacity, sides,

time: 64.2 us -> 60.7 us (0.945)
  Pallas kernels: 63.4 us -> 59.9 us
    pallas_call x1, Pallas kernels: 61.5 us -> 58.1 us  [layer(): pl.pallas_call(functools.partial(layer_kernel, groups, capacity), out_sha...]
where the time goes in v6:
time: 60.7 us; the launch traced here: 60.6 us
  Pallas kernels  59.9 us (99%)
  between operations  0.64 us (1%)
    pallas_call x1, Pallas kernels, layer(): pl.pallas_call(functools.partial(layer_kernel, groups, capacity), out_sha...  58.1 us
    pallas_call x1, Pallas kernels, layer(): pl.pallas_call(settle_kernel, out_shape=[jax.ShapeDtypeStruct(tokens.shap...  1.88 us

profile of v6, /device:TPU:0, one launch (start us, length us, event | category | flops | bytes accessed | tf_op | source)
XLA Modules:
  0.0 60.6 jit_solution(7389845182497250214)
XLA Ops:
  0.6 58.1 %layer.1 = (bf16[2,192,512]{2,1,0:T(8,128)(2,1)}, bf16[128,192]{1,0:T(8,128)(2,1)}) custom-call(bf16[128,512]{1,0:T(8,128)(2,1)} %tokens_ref.1, s32[1,128]{1,0:T(1,128)} %bitcast.7, bf16[128,512]{1,0:T(8,128)(2,1)} %cotangent_hbm.1, s32[16,16,100]{2,1,0:T(8,128)} %bitcast.5, s32[16,16,100]{2,1,0:T(8,128)} %bitcast.6, bf16[2048,2048]{1,0:T(8,128)(2,1)} %wu_hbm.1, ...), custom_call_target="tpu_custom_call" | custom-call | tf_op jit(solution)/shard_map/layer/pallas_call | solution.py:439
  58.7 1.9 %settle.1 = (bf16[128,512]{1,0:T(8,128)(2,1)}, bf16[128,512]{1,0:T(8,128)(2,1)}) custom-call(bf16[2,192,512]{2,1,0:T(8,128)(2,1)} %get-tuple-element.4.rows_ref, bf16[128,192]{1,0:T(8,128)(2,1)} %get-tuple-element.5.turned_ref), custom_call_target="tpu_custom_call" | custom-call | tf_op jit(solution)/shard_map/settle/pallas_call | solution.py:480

commit v7 on v6

--- a/solution.py
+++ b/solution.py
@@ -250,7 +250,6 @@
     arrive(trip_a)
     share_a = share(got_a, base)
     trip_b = dispatch(send_b, got_b, 2 * step)
-    steps(0, half, 2, lambda f: expand(down_ref[f], ed_ref, f))
     arrive(share_a[:1])
     forward_a = forward(got_a, base)
     arrive(share_a[1:] + forward_a)
@@ -274,9 +273,9 @@
         slope_ref[:, columns(f)] = slope
 
     def pre_pair(f):
-        expand(down_ref[half + f // 2], ed_ref, half + f // 2)
-        pre_step(f)
-        pre_step(f + 1)
+        for n in range(2):
+            expand(down_ref[f + n], ed_ref, f + n)
+            pre_step(f + n)
 
     def grad_step(f):
         grad = dot(g_ref[...] * ed_ref[f], wd_ref[columns(f), :], NT)

time: 60.7 us -> 61.9 us (1.020)
  Pallas kernels: 59.9 us -> 61.1 us
    pallas_call x1, Pallas kernels: 58.1 us -> 59.3 us  [layer(): pl.pallas_call(functools.partial(layer_kernel, groups, capacity), out_sha...]
where the time goes in v7:
time: 61.9 us; the launch traced here: 61.8 us
  Pallas kernels  61.1 us (99%)
  between operations  0.64 us (1%)
    pallas_call x1, Pallas kernels, layer(): pl.pallas_call(functools.partial(layer_kernel, groups, capacity), out_sha...  59.3 us
    pallas_call x1, Pallas kernels, layer(): pl.pallas_call(settle_kernel, out_shape=[jax.ShapeDtypeStruct(tokens.shap...  1.88 us

profile of v7, /device:TPU:0, one launch (start us, length us, event | category | flops | bytes accessed | tf_op | source)
XLA Modules:
  0.0 61.8 jit_solution(4452934016618863141)
XLA Ops:
  0.6 59.3 %layer.1 = (bf16[2,192,512]{2,1,0:T(8,128)(2,1)}, bf16[128,192]{1,0:T(8,128)(2,1)}) custom-call(bf16[128,512]{1,0:T(8,128)(2,1)} %tokens_ref.1, s32[1,128]{1,0:T(1,128)} %bitcast.7, bf16[128,512]{1,0:T(8,128)(2,1)} %cotangent_hbm.1, s32[16,16,100]{2,1,0:T(8,128)} %bitcast.5, s32[16,16,100]{2,1,0:T(8,128)} %bitcast.6, bf16[2048,2048]{1,0:T(8,128)(2,1)} %wu_hbm.1, ...), custom_call_target="tpu_custom_call" | custom-call | tf_op jit(solution)/shard_map/layer/pallas_call | solution.py:438
  59.9 1.9 %settle.1 = (bf16[128,512]{1,0:T(8,128)(2,1)}, bf16[128,512]{1,0:T(8,128)(2,1)}) custom-call(bf16[2,192,512]{2,1,0:T(8,128)(2,1)} %get-tuple-element.4.rows_ref, bf16[128,192]{1,0:T(8,128)(2,1)} %get-tuple-element.5.turned_ref), custom_call_target="tpu_custom_call" | custom-call | tf_op jit(solution)/shard_map/settle/pallas_call | solution.py:479
